TPU v7x, 256 devices: a whole 4x4x8 slice. The times are simulated.
256 devices in a mesh: gx: 16 (over x_hi, z), gy: 4 (over x_lo, core), gz: 4 (over y).
Axes of the slice: x: 4 (x_hi: 2, x_lo: 2; x = x_hi * 2 + x_lo), y: 4, z: 8, core: 2. Of those that a mesh axis runs over, the one named last changes fastest.
Arguments:
- fine_params: float32 [16, 8, 8, 8704], P('gx', 'gy', 'gz'), may hold values from -0.75 to 0.75
- coarse_inner: float32 [5, 512], replicated, may hold values from -4 to 4
- coarse_outer: float32 [512], replicated, may hold values from -0.25 to 0.25
- points: float32 [16, 8, 8, 4, 128], P('gx', 'gy', 'gz'), may hold values from -1 to 1
- source: float32 [16, 8, 8, 128], P('gx', 'gy', 'gz'), may hold values from -6 to 6
- conductivity: float32 [16, 8, 8], P('gx', 'gy', 'gz'), may hold values from 0.3 to 3
- face_points: int32 [16, 8, 8, 6, 32], P('gx', 'gy', 'gz'), may hold values from 0 to 127, as said below
Outputs:
- residual: float32 [16, 8, 8, 128], P('gx', 'gy', 'gz')
- fine_grads: float32 [16, 8, 8, 8704], P('gx', 'gy', 'gz')
- coarse_inner_grads: float32 [5, 512], replicated
- coarse_outer_grads: float32 [512], replicated
Inputs may be any that keep to these rules, and one draw needn't show every extreme that they name: Each row face_points[a, b, c, d, :] holds 32 distinct point numbers.
All inputs are finite; a program needn't handle non-finite values.
Results may differ from a plain program's by a relative error of at most 0.0003.
Values sent between devices are 32-bit elements; how exact they have to be, the bound alone decides.
A program may use at most 192 MiB of HBM per device.

v0:
```python
from functools import partial

import jax
import jax.numpy as jnp
from jax import lax
from jax.experimental import pallas as pl
from jax.experimental.pallas import tpu as pltpu
from jax.sharding import PartitionSpec as P

PTS = 128
FACE = 32
HID = 64
COARSE = 512
ROWS = 68
NETS = 4
CH = 6
WIDTH = CH * PTS
AXES = ("gx", "gy", "gz")
MESH = pl.DeviceIdType.MESH
BF = jnp.bfloat16
F32 = jnp.float32


def split2(x):
    hi = x.astype(BF)
    return hi, (x - hi.astype(F32)).astype(BF)


def split3(x):
    hi = x.astype(BF)
    rest = x - hi.astype(F32)
    mid = rest.astype(BF)
    return hi, mid, (rest - mid.astype(F32)).astype(BF)


def dot(a, b):
    return lax.dot_general(a, b, (((1,), (0,)), ((), ())), preferred_element_type=F32)


def dot_nt(a, b):
    return lax.dot_general(a, b, (((1,), (1,)), ((), ())), preferred_element_type=F32)


def iota(shape, dim):
    return lax.broadcasted_iota(jnp.int32, shape, dim)


def stacked3(row):
    which = iota((16, row.shape[1]), 0)
    hi = row.astype(BF).astype(F32)
    rest = row - hi
    mid = rest.astype(BF).astype(F32)
    low = rest - mid
    rows = jnp.where(which == 0, hi, jnp.where(which == 1, mid, jnp.where(which == 2, low, 0.0)))
    return rows.astype(BF)


def coefficients(x):
    sx, sy, sz, kappa = x[0:1], x[1:2], x[2:3], x[4:5]
    square = sx * sx + sy * sy + sz * sz
    window = jnp.exp(-square)
    scaled = kappa * window
    return (
        scaled * (6.0 - 4.0 * square),
        4.0 * scaled * sx,
        4.0 * scaled * sy,
        4.0 * scaled * sz,
        2.0 * window,
        -scaled,
    )


def kernel(
    sizes,
    params,
    inner,
    outer,
    points,
    source,
    kappa,
    faces,
    res_out,
    grad_out,
    coarse_out,
    hot,
    gbuf,
    gin,
    ebuf,
    ein,
    rbuf,
    rin,
    xs,
    cols,
    wide,
    wsq,
    lf,
    lb,
    act1,
    act2,
    hid1,
    state2,
    dlast,
    qs,
    dz,
    acc3,
    acc2,
    acc1,
    acco,
    work,
    eown,
    ecoarse,
    ccols,
    cact,
    cvec,
    ar,
    g_send,
    g_recv,
    e_send,
    e_recv,
    r_send,
    r_recv,
    ar_send,
    ar_recv,
):
    place = [lax.axis_index(axis) for axis in AXES]

    def target(slot, flip):
        axis = slot // 2
        sign = (2 * (slot % 2) - 1) * (-1 if flip else 1)
        return AXES[axis], place[axis] + sign, sizes[axis]

    low = min(4, sizes[0])
    groups = [
        ("gy", place[1], sizes[1], lambda p: p),
        ("gz", place[2], sizes[2], lambda p: p),
        ("gx", place[0] % low, low, lambda p: (place[0] // low) * low + p),
        ("gx", place[0] // low, sizes[0] // low, lambda p: p * low + place[0] % low),
    ]

    def exchange(source_of, landing, send_sem, recv_sem, flip):
        for slot in range(6):
            axis, where, size = target(slot, flip)

            @pl.when(jnp.logical_and(where >= 0, where < size))
            def _(slot=slot, axis=axis, where=where):
                pltpu.make_async_remote_copy(
                    source_of(slot), landing.at[slot], send_sem.at[slot], recv_sem.at[slot],
                    device_id={axis: where}, device_id_type=MESH,
                ).start()

    def arrive(source_of, landing, send_sem, recv_sem, flip):
        for slot in range(6):
            axis, where, size = target(slot, not flip)

            @pl.when(jnp.logical_and(where >= 0, where < size))
            def _(slot=slot, axis=axis, where=where):
                pltpu.make_async_remote_copy(
                    source_of(slot), landing.at[slot], send_sem.at[slot], recv_sem.at[slot],
                    device_id={axis: where}, device_id_type=MESH,
                ).wait_recv()

    def sent(source_of, landing, send_sem, recv_sem, flip):
        for slot in range(6):
            axis, where, size = target(slot, flip)

            @pl.when(jnp.logical_and(where >= 0, where < size))
            def _(slot=slot, axis=axis, where=where):
                pltpu.make_async_remote_copy(
                    source_of(slot), landing.at[slot], send_sem.at[slot], recv_sem.at[slot],
                    device_id={axis: where}, device_id_type=MESH,
                ).wait_send()

    def ar_copies(stage, arriving):
        axis, pos, size, member = groups[stage]
        for k in range(1, size):
            partner = lax.rem(pos + k, size)
            slot = partner if arriving else pos
            yield pltpu.make_async_remote_copy(
                ar.at[stage, pos], ar.at[stage, slot],
                ar_send.at[stage, partner], ar_recv.at[stage, slot],
                device_id={axis: member(partner)}, device_id_type=MESH,
            )

    def ar_start(stage, value):
        ar[stage, groups[stage][1]] = value
        for out in ar_copies(stage, False):
            out.start()

    def ar_finish(stage):
        for back in ar_copies(stage, True):
            back.wait_recv()
        total = ar[stage, 0]
        for p in range(1, groups[stage][2]):
            total = total + ar[stage, p]
        return total

    gin[...] = jnp.zeros_like(gin)
    ein[...] = jnp.zeros_like(ein)
    rin[...] = jnp.zeros_like(rin)

    barrier = pltpu.get_barrier_semaphore()
    expected = 0
    for slot in (0, 1):
        axis, where, size = target(slot, False)
        present = jnp.logical_and(where >= 0, where < size)

        @pl.when(present)
        def _(axis=axis, where=where):
            pl.semaphore_signal(barrier, inc=1, device_id={axis: where}, device_id_type=MESH)

        expected = expected + jnp.where(present, 1, 0)
    for axis, pos, size, member in groups:
        for k in range(1, size):
            pl.semaphore_signal(
                barrier, inc=1, device_id={axis: member(lax.rem(pos + k, size))}, device_id_type=MESH
            )
        expected = expected + (size - 1)

    lane = iota((1, PTS), 1)
    row8 = iota((8, PTS), 0)
    group = lane // FACE
    for j in range(NETS):
        b, c = j // 2, j % 2
        index = faces[j]
        first = jnp.concatenate([index[k : k + 1] for k in range(4)], axis=1)
        second = jnp.concatenate(
            [index[4:5], index[5:6], jnp.full((1, 2 * FACE), -1, jnp.int32)], axis=1
        )
        point = iota((PTS, PTS), 0)
        hot[j, :, 0:PTS] = jnp.where(point == first, 1.0, 0.0).astype(BF)
        hot[j, :, PTS : 2 * PTS] = jnp.where(point == second, 1.0, 0.0).astype(BF)
        own = jnp.concatenate([points[j], jnp.zeros((4, PTS), F32)], axis=0)
        own = jnp.where(row8 == 4, kappa[b, c], own)
        xs[j, 0] = own
        hi, mid, low_part = split3(own)
        pieces = jnp.concatenate([hi, mid, low_part, jnp.zeros_like(hi)], axis=0)
        moved = dot(pieces, hot[j])
        moved = moved[0:8] + moved[8:16] + moved[16:24]
        shift_a = jnp.where(row8 == group // 2, (2 * (group % 2) - 1).astype(F32), 0.0)
        shift_b = jnp.where(row8 == 2, jnp.where(group < 2, (2 * (group % 2) - 1).astype(F32), 0.0), 0.0)
        gbuf[0, j] = moved[:, 0:PTS] - shift_a
        gbuf[1, j] = moved[:, PTS : 2 * PTS] - shift_b

    pl.semaphore_wait(barrier, expected)
    g_args = (lambda slot: gbuf.at[slot // 4], gin, g_send, g_recv, False)
    exchange(*g_args)

    half = iota((32, PTS), 1) < HID
    for n in range(NETS):
        flat = params[n]
        even = pltpu.roll(jnp.where(half, flat[35:67], flat[2:34]), HID, 1)
        odd = jnp.where(half, flat[3:35], flat[35:67])
        work[pl.ds(0, 32, stride=2), :] = even
        work[pl.ds(1, 32, stride=2), :] = odd
        both = work[...]
        hi, lo = split2(both)
        lb[n, 0, :, 0:64] = hi[:, 0:64]
        lb[n, 0, :, 64:128] = hi[:, 0:64]
        lb[n, 0, :, 128:192] = lo[:, 0:64]
        lb[n, 1, :, 0:64] = hi[:, 64:128]
        lb[n, 1, :, 64:128] = hi[:, 64:128]
        lb[n, 1, :, 128:192] = lo[:, 64:128]
        hi, lo = split2(both.T)
        for layer in range(2):
            lf[n, layer, :, 0:64] = hi[64 * layer : 64 * layer + 64]
            lf[n, layer, :, 64:128] = hi[64 * layer : 64 * layer + 64]
            lf[n, layer, :, 128:192] = lo[64 * layer : 64 * layer + 64]
        vectors = jnp.concatenate(
            [
                flat[0:1],
                pltpu.roll(flat[0:1], HID, 1),
                flat[1:2],
                pltpu.roll(flat[1:2], HID, 1),
                flat[2:3],
                pltpu.roll(flat[34:35], HID, 1),
                flat[67:68],
                pltpu.roll(flat[67:68], HID, 1),
            ],
            axis=0,
        )
        columns = vectors.T
        for k in range(8):
            wide[n, k] = jnp.broadcast_to(columns[0:64, k : k + 1], (64, PTS))
        wsq[n] = wide[n, 0] * wide[n, 0] + wide[n, 1] * wide[n, 1] + wide[n, 2] * wide[n, 2]
        first_channel = jnp.where(
            jnp.logical_and(iota((16, PTS), 0) == 0, iota((16, PTS), 1) >= 0), 1.0, 0.0
        ).astype(BF)
        for tile in range(3):
            for k in range(CH):
                at = (tile * CH + k) * PTS
                value = first_channel if k == 0 else jnp.zeros_like(first_channel)
                act1[n, 192:208, at : at + PTS] = value
                act2[n, 192:208, at : at + PTS] = value

    def put(ref, n, at, value):
        hi, lo = split2(value)
        ref[n, 0:64, at : at + PTS] = hi
        ref[n, 64:128, at : at + PTS] = lo
        ref[n, 128:192, at : at + PTS] = hi

    def forward(n, tiles):
        begin, end = tiles[0] * WIDTH, (tiles[-1] + 1) * WIDTH
        for tile in tiles:
            x = xs[n, tile]
            pre = (
                wide[n, 4]
                + wide[n, 0] * x[0:1]
                + wide[n, 1] * x[1:2]
                + wide[n, 2] * x[2:3]
                + wide[n, 3] * x[3:4]
            )
            hidden = jnp.tanh(pre)
            one = 1.0 - hidden * hidden
            two = -2.0 * hidden * one
            hid1[n, :, tile * PTS : (tile + 1) * PTS] = hidden
            at = tile * WIDTH
            put(act1, n, at, hidden)
            for k in range(4):
                put(act1, n, at + (k + 1) * PTS, one * wide[n, k])
            put(act1, n, at + 5 * PTS, two * wsq[n])
        product = dot(lf[n, 0], act1[n, 0:192, begin:end])
        for tile in tiles:
            at = tile * WIDTH
            z = [product[:, at - begin + k * PTS : at - begin + (k + 1) * PTS] for k in range(CH)]
            hidden = jnp.tanh(z[0] + wide[n, 5])
            one = 1.0 - hidden * hidden
            two = -2.0 * hidden * one
            state2[n, :, at : at + PTS] = hidden
            for k in range(1, CH):
                state2[n, :, at + k * PTS : at + (k + 1) * PTS] = z[k]
            put(act2, n, at, hidden)
            for k in range(1, 5):
                put(act2, n, at + k * PTS, one * z[k])
            put(act2, n, at + 5 * PTS, two * (z[1] * z[1] + z[2] * z[2] + z[3] * z[3]) + one * z[5])
        product = dot(lf[n, 1], act2[n, 0:192, begin:end])
        results = []
        for tile in tiles:
            at = tile * WIDTH
            z = [product[:, at - begin + k * PTS : at - begin + (k + 1) * PTS] for k in range(CH)]
            coef = coefficients(xs[n, tile])
            hidden = jnp.tanh(z[0] + wide[n, 6])
            squared = hidden * hidden
            one = 1.0 - squared
            two = -2.0 * hidden * one
            three = -2.0 * one * (1.0 - 3.0 * squared)
            mixed = coef[5] * z[5]
            for k in range(1, 5):
                mixed = mixed + coef[k] * z[k]
            curved = coef[5] * (z[1] * z[1] + z[2] * z[2] + z[3] * z[3])
            q = coef[0] * hidden + one * mixed + two * curved
            hi, lo = split2(q)
            qs[n, 0:64, tile * PTS : (tile + 1) * PTS] = hi
            qs[n, 64:128, tile * PTS : (tile + 1) * PTS] = lo
            out = wide[n, 7]
            results.append(jnp.sum(out * q, axis=0, keepdims=True))
            one, two, three = out * one, out * two, out * three
            twice = 2.0 * coef[5] * two
            dlast[n, :, at : at + PTS] = coef[0] * one + two * mixed + three * curved
            for k in range(1, 4):
                dlast[n, :, at + k * PTS : at + (k + 1) * PTS] = coef[k] * one + twice * z[k]
            dlast[n, :, at + 4 * PTS : at + 5 * PTS] = coef[4] * one
            dlast[n, :, at + 5 * PTS : at + 6 * PTS] = coef[5] * one
        return results

    def backward(n, tiles, rows, add):
        begin, end = tiles[0] * WIDTH, (tiles[-1] + 1) * WIDTH

        def collect(ref, value):
            ref[n] = ref[n] + value if add else value

        for tile, row in zip(tiles, rows):
            for k in range(CH):
                at = tile * WIDTH + k * PTS
                put(dz, 0, at, dlast[n, :, at : at + PTS] * row)
        product = dot(lb[n, 1], dz[0, 0:192, begin:end])
        collect(acc3, dot_nt(act2[n, 64:208, begin:end], dz[0, 0:128, begin:end]))
        row = jnp.concatenate(rows, axis=1)
        span = slice(tiles[0] * PTS, (tiles[-1] + 1) * PTS)
        collect(acco, dot_nt(stacked3(row), qs[n, :, span]))
        for tile in tiles:
            at = tile * WIDTH
            a = [product[:, at - begin + k * PTS : at - begin + (k + 1) * PTS] for k in range(CH)]
            z = [state2[n, :, at + k * PTS : at + (k + 1) * PTS] for k in range(CH)]
            squared = z[0] * z[0]
            one = 1.0 - squared
            two = -2.0 * z[0] * one
            three = -2.0 * one * (1.0 - 3.0 * squared)
            mixed = z[5] * a[5]
            for k in range(1, 5):
                mixed = mixed + z[k] * a[k]
            curved = (z[1] * z[1] + z[2] * z[2] + z[3] * z[3]) * a[5]
            put(dz, 1, at, one * a[0] + two * mixed + three * curved)
            twice = 2.0 * two * a[5]
            for k in range(1, 4):
                put(dz, 1, at + k * PTS, one * a[k] + twice * z[k])
            put(dz, 1, at + 4 * PTS, one * a[4])
            put(dz, 1, at + 5 * PTS, one * a[5])
        product = dot(lb[n, 0], dz[1, 0:192, begin:end])
        collect(acc2, dot_nt(act1[n, 64:208, begin:end], dz[1, 0:128, begin:end]))
        total = None
        for tile in tiles:
            at = tile * WIDTH
            a = [product[:, at - begin + k * PTS : at - begin + (k + 1) * PTS] for k in range(CH)]
            hidden = hid1[n, :, tile * PTS : (tile + 1) * PTS]
            squared = hidden * hidden
            one = 1.0 - squared
            two = -2.0 * hidden * one
            three = -2.0 * one * (1.0 - 3.0 * squared)
            mixed = wide[n, 0] * a[1]
            for k in range(1, 4):
                mixed = mixed + wide[n, k] * a[k + 1]
            twice = 2.0 * two * a[5]
            base = tile * WIDTH
            put(dz, 2, base, one * a[0] + two * mixed + three * (wsq[n] * a[5]))
            for k in range(3):
                put(dz, 2, base + (k + 1) * PTS, one * a[k + 1] + twice * wide[n, k])
            put(dz, 2, base + 4 * PTS, one * a[4])
            x = xs[n, tile]
            hi = x.astype(BF).astype(F32)
            top = jnp.where(row8 < 4, hi, jnp.where(row8 == 4, 1.0, 0.0))
            bottom = jnp.where(row8 < 4, x - hi, 0.0)
            pieces = [jnp.concatenate([top, bottom], axis=0)]
            for k in range(4):
                pieces.append(jnp.where(iota((16, PTS), 0) == k, 1.0, 0.0))
            left = jnp.concatenate(pieces, axis=1).astype(BF)
            part = dot_nt(left, dz[2, 0:128, base : base + 5 * PTS])
            total = part if total is None else total + part
        collect(acc1, total)

    def own_forward(n, carry):
        eown[n] = jnp.broadcast_to(forward(n, (0,))[0], (8, PTS))
        return carry

    lax.fori_loop(0, NETS, own_forward, 0)

    arrive(*g_args)
    def choose(parts):
        picked = parts[-1]
        for k in range(len(parts) - 2, -1, -1):
            picked = jnp.where(group == k, parts[k], picked)
        return picked

    blank = jnp.zeros((8, PTS), F32)
    for n in range(NETS):
        b, c = n // 2, n % 2
        slots = [
            gin[0, n],
            gin[1, n],
            gbuf[0, n + 2] if b == 0 else gin[2, n - 2],
            gbuf[0, n - 2] if b == 1 else gin[3, n + 2],
        ]
        xs[n, 1] = choose(slots)
        slots = [
            gbuf[1, n + 1] if c == 0 else gin[4, n - 1],
            gbuf[1, n - 1] if c == 1 else gin[5, n + 1],
            blank,
        ]
        xs[n, 2] = choose(slots)

    def face_forward(n, carry):
        first, second = forward(n, (1, 2))
        ebuf[0, pl.ds(n, 1), :] = first
        ebuf[1, pl.ds(n, 1), :] = second
        return carry

    ebuf[...] = jnp.zeros_like(ebuf)
    lax.fori_loop(0, NETS, face_forward, 0)
    e_args = (lambda slot: ebuf.at[slot // 4], ein, e_send, e_recv, True)
    exchange(*e_args)

    scales = (2.0 / sizes[0], 2.0 / (2 * sizes[1]), 2.0 / (2 * sizes[2]))
    ci = inner[...]
    co = outer[...]
    squares = (
        ci[0:1] * ci[0:1] * (scales[0] * scales[0])
        + ci[1:2] * ci[1:2] * (scales[1] * scales[1])
        + ci[2:3] * ci[2:3] * (scales[2] * scales[2])
    )
    pad = jnp.zeros((3, COARSE), F32)
    c8 = jnp.concatenate([ci, pad], axis=0)
    hi = c8.astype(BF).astype(F32)
    mid = (c8 - hi).astype(BF).astype(F32)
    lo = c8 - hi - mid
    fronts = jnp.concatenate([hi, hi, mid, hi, lo, mid], axis=0).T.astype(BF)
    two_rows = jnp.concatenate(
        [2.0 * co * ci[3:4], 2.0 * co * squares, jnp.zeros((6, COARSE), F32)], axis=0
    ).T
    ccols[0] = jnp.broadcast_to(two_rows[:, 0:1], (COARSE, PTS))
    ccols[1] = jnp.broadcast_to(two_rows[:, 1:2], (COARSE, PTS))
    for j in range(NETS):
        b, c = j // 2, j % 2
        centres = (
            place[0].astype(F32) + 0.5,
            (2 * place[1] + b).astype(F32) + 0.5,
            (2 * place[2] + c).astype(F32) + 0.5,
        )
        own = xs[j, 0]
        v = jnp.where(row8 == 3, own, 0.0)
        for k in range(3):
            v = jnp.where(row8 == k, (centres[k] + own) * scales[k] - 1.0, v)
        v = jnp.where(row8 == 4, 1.0, v)
        cvec[j] = v
        hi = v.astype(BF).astype(F32)
        mid = (v - hi).astype(BF).astype(F32)
        lo = v - hi - mid
        backs = jnp.concatenate([hi, mid, hi, lo, hi, mid], axis=0).astype(BF)
        hidden = jnp.tanh(dot(fronts, backs))
        squared = hidden * hidden
        one = 1.0 - squared
        curve = one * hidden
        bend = one * (1.0 - 3.0 * squared)
        ecoarse[j : j + 1, :] = jnp.sum(
            ccols[0] * one + ccols[1] * (curve * kappa[b, c]), axis=0, keepdims=True
        )
        for k, value in enumerate((curve, bend, one)):
            hi, lo = split2(value)
            cact[2 * k, :, j * PTS : (j + 1) * PTS] = hi
            cact[2 * k + 1, :, j * PTS : (j + 1) * PTS] = lo

    arrive(*e_args)
    for j in range(NETS):
        b, c = j // 2, j % 2

        def row(ref, k):
            return ref[k : k + 1, :]

        first = choose(
            [
                row(ein.at[0], j),
                row(ein.at[1], j),
                row(ebuf.at[0], j - 2) if b == 1 else row(ein.at[2], j + 2),
                row(ebuf.at[0], j + 2) if b == 0 else row(ein.at[3], j - 2),
            ]
        )
        second = choose(
            [
                row(ebuf.at[1], j - 1) if c == 1 else row(ein.at[4], j + 1),
                row(ebuf.at[1], j + 1) if c == 0 else row(ein.at[5], j - 1),
                jnp.zeros((1, PTS), F32),
            ]
        )
        spread = dot_nt(stacked3(jnp.concatenate([first, second], axis=1)), hot[j])
        fine = eown[j, 0:1, :] + spread[0:1] + spread[1:2] + spread[2:3]
        residual = fine + ecoarse[j : j + 1, :] - source[j : j + 1, :]
        res_out[j : j + 1, :] = residual
        scaled = residual * (1.0 / PTS)
        eown[j] = jnp.broadcast_to(scaled, (8, PTS))
        moved = dot(stacked3(scaled), hot[j])
        moved = moved[0:1] + moved[1:2] + moved[2:3]
        rbuf[0, j : j + 1, :] = moved[:, 0:PTS]
        rbuf[1, j : j + 1, :] = moved[:, PTS : 2 * PTS]
    rbuf[:, 4:8, :] = jnp.zeros((2, 4, PTS), F32)
    r_args = (lambda slot: rbuf.at[slot // 4], rin, r_send, r_recv, False)
    exchange(*r_args)

    blocks = []
    for j in range(NETS):
        b, c = j // 2, j % 2
        plain = eown[j] * cvec[j]
        plain = jnp.concatenate([plain, plain * kappa[b, c]], axis=0)
        hi = plain.astype(BF).astype(F32)
        blocks.append(jnp.concatenate([hi, plain - hi], axis=0))
    left = jnp.concatenate(blocks, axis=1).astype(BF)
    sums = []
    for k in range(3):
        upper = dot_nt(left, cact[2 * k])
        lower = dot_nt(left, cact[2 * k + 1])
        sums.append(upper[0:16] + upper[16:32] + lower[0:16])
    s_one, s_curve = sums[2][4:5], sums[0][12:13]
    moments = co * (2.0 * squares * sums[1][8:13] - 4.0 * ci[3:4] * sums[0][0:5])
    extra = jnp.concatenate(
        [
            (4.0 * scales[0] * scales[0]) * ci[0:1] * co * s_curve,
            (4.0 * scales[1] * scales[1]) * ci[1:2] * co * s_curve,
            (4.0 * scales[2] * scales[2]) * ci[2:3] * co * s_curve,
            2.0 * co * s_one,
            jnp.zeros((1, COARSE), F32),
        ],
        axis=0,
    )
    outer_grad = 2.0 * ci[3:4] * s_one + 2.0 * squares * s_curve
    partial_sums = jnp.concatenate(
        [moments + extra, outer_grad, jnp.zeros((2, COARSE), F32)], axis=0
    )
    ar_start(0, partial_sums)

    def own_backward(n, carry):
        backward(n, (0,), [eown[n, 0:1, :]], False)
        return carry

    lax.fori_loop(0, 2, own_backward, 0)
    ar_start(1, ar_finish(0))
    lax.fori_loop(2, NETS, own_backward, 0)
    ar_start(2, ar_finish(1))

    arrive(*r_args)
    for n in range(NETS):
        b, c = n // 2, n % 2
        first = choose(
            [
                rin[0, n : n + 1, :],
                rin[1, n : n + 1, :],
                rbuf[0, n + 2 : n + 3, :] if b == 0 else rin[2, n - 2 : n - 1, :],
                rbuf[0, n - 2 : n - 1, :] if b == 1 else rin[3, n + 2 : n + 3, :],
            ]
        )
        second = choose(
            [
                rbuf[1, n + 1 : n + 2, :] if c == 0 else rin[4, n - 1 : n, :],
                rbuf[1, n - 1 : n, :] if c == 1 else rin[5, n + 1 : n + 2, :],
                jnp.zeros((1, PTS), F32),
            ]
        )
        cols[n, 0] = jnp.broadcast_to(first, (8, PTS))
        cols[n, 1] = jnp.broadcast_to(second, (8, PTS))

    def face_backward(n, carry):
        backward(n, (1, 2), [cols[n, 0, 0:1, :], cols[n, 1, 0:1, :]], True)
        joined = []
        for ref in (acc2, acc3):
            low_rows = ref[n, 0:64, :]
            high_rows = ref[n, 64:128, :]
            joined.append(low_rows[:, 0:64] + high_rows[:, 0:64] + high_rows[:, 64:128])
        work[...] = jnp.concatenate(joined, axis=1)
        even = work[pl.ds(0, 32, stride=2), :]
        odd = work[pl.ds(1, 32, stride=2), :]
        bias2 = acc2[n, 128:129, :]
        bias3 = acc3[n, 128:129, :]
        bias2 = bias2[:, 0:64] + bias2[:, 64:128]
        bias3 = bias3[:, 0:64] + bias3[:, 64:128]
        first = acc1[n, 0:8, :] + acc1[n, 8:16, :]
        first = first[:, 0:64] + first[:, 64:128]
        last = acco[n, 0:1, :] + acco[n, 1:2, :] + acco[n, 2:3, :]
        last = last[:, 0:64] + last[:, 64:128]
        grad_out[n, 0:1, 0:64] = first[0:1]
        grad_out[n, 0:1, 64:128] = first[1:2]
        grad_out[n, 1:2, 0:64] = first[2:3]
        grad_out[n, 1:2, 64:128] = first[3:4]
        grad_out[n, 2:3, 0:64] = first[4:5]
        grad_out[n, 2:34, 64:128] = even[:, 0:64]
        grad_out[n, 3:35, 0:64] = odd[:, 0:64]
        grad_out[n, 34:35, 64:128] = bias2
        grad_out[n, 35:67, 0:64] = even[:, 64:128]
        grad_out[n, 35:67, 64:128] = odd[:, 64:128]
        grad_out[n, 67:68, 0:64] = bias3
        grad_out[n, 67:68, 64:128] = last
        return carry

    lax.fori_loop(0, 2, face_backward, 0)
    ar_start(3, ar_finish(2))
    lax.fori_loop(2, NETS, face_backward, 0)
    count = NETS * sizes[0] * sizes[1] * sizes[2]
    coarse_out[...] = ar_finish(3) * (count ** (-0.5))

    for args in (g_args, e_args, r_args):
        sent(*args)
    for stage in range(4):
        for out in ar_copies(stage, False):
            out.wait_send()


def on_device(fine_params, coarse_inner, coarse_outer, points, source, conductivity, face_points):
    sizes = tuple(lax.axis_size(axis) for axis in AXES)
    vmem = pl.BlockSpec(memory_space=pltpu.VMEM)
    smem = pl.BlockSpec(memory_space=pltpu.SMEM)
    residual, grads, coarse = pl.pallas_call(
        partial(kernel, sizes),
        out_shape=(
            jax.ShapeDtypeStruct((NETS, PTS), F32),
            jax.ShapeDtypeStruct((NETS, ROWS, PTS), F32),
            jax.ShapeDtypeStruct((8, COARSE), F32),
        ),
        in_specs=[vmem, vmem, vmem, vmem, vmem, smem, vmem],
        out_specs=(vmem, vmem, vmem),
        scratch_shapes=[
            pltpu.VMEM((NETS, PTS, 2 * PTS), BF),
            pltpu.VMEM((2, NETS, 8, PTS), F32),
            pltpu.VMEM((6, NETS, 8, PTS), F32),
            pltpu.VMEM((2, 8, PTS), F32),
            pltpu.VMEM((6, 8, PTS), F32),
            pltpu.VMEM((2, 8, PTS), F32),
            pltpu.VMEM((6, 8, PTS), F32),
            pltpu.VMEM((NETS, 3, 8, PTS), F32),
            pltpu.VMEM((NETS, 2, 8, PTS), F32),
            pltpu.VMEM((NETS, 8, HID, PTS), F32),
            pltpu.VMEM((NETS, HID, PTS), F32),
            pltpu.VMEM((NETS, 2, HID, 3 * HID), BF),
            pltpu.VMEM((NETS, 2, HID, 3 * HID), BF),
            pltpu.VMEM((NETS, 208, 3 * WIDTH), BF),
            pltpu.VMEM((NETS, 208, 3 * WIDTH), BF),
            pltpu.VMEM((NETS, HID, 3 * PTS), F32),
            pltpu.VMEM((NETS, HID, 3 * WIDTH), F32),
            pltpu.VMEM((NETS, HID, 3 * WIDTH), F32),
            pltpu.VMEM((NETS, PTS, 3 * PTS), BF),
            pltpu.VMEM((3, 192, 3 * WIDTH), BF),
            pltpu.VMEM((NETS, 144, PTS), F32),
            pltpu.VMEM((NETS, 144, PTS), F32),
            pltpu.VMEM((NETS, 16, PTS), F32),
            pltpu.VMEM((NETS, 16, PTS), F32),
            pltpu.VMEM((HID, PTS), F32),
            pltpu.VMEM((NETS, 8, PTS), F32),
            pltpu.VMEM((8, PTS), F32),
            pltpu.VMEM((2, COARSE, PTS), F32),
            pltpu.VMEM((6, COARSE, NETS * PTS), BF),
            pltpu.VMEM((NETS, 8, PTS), F32),
            pltpu.VMEM((4, 4, 8, COARSE), F32),
            pltpu.SemaphoreType.DMA((6,)),
            pltpu.SemaphoreType.DMA((6,)),
            pltpu.SemaphoreType.DMA((6,)),
            pltpu.SemaphoreType.DMA((6,)),
            pltpu.SemaphoreType.DMA((6,)),
            pltpu.SemaphoreType.DMA((6,)),
            pltpu.SemaphoreType.DMA((4, 4)),
            pltpu.SemaphoreType.DMA((4, 4)),
        ],
        compiler_params=pltpu.CompilerParams(
            collective_id=0, has_side_effects=True, vmem_limit_bytes=48 * 1024 * 1024
        ),
    )(
        fine_params.reshape(NETS, ROWS, PTS),
        coarse_inner,
        coarse_outer.reshape(1, COARSE),
        points.reshape(NETS, 4, PTS),
        source.reshape(NETS, PTS),
        conductivity.reshape(2, 2),
        face_points.reshape(NETS, 6, FACE),
    )
    return (
        residual.reshape(source.shape),
        grads.reshape(fine_params.shape),
        coarse[0:5],
        coarse[5],
    )


def solution(mesh):
    return jax.shard_map(
        on_device,
        mesh=mesh,
        in_specs=(
            P("gx", "gy", "gz", None),
            P(),
            P(),
            P("gx", "gy", "gz", None, None),
            P("gx", "gy", "gz", None),
            P("gx", "gy", "gz"),
            P("gx", "gy", "gz", None, None),
        ),
        out_specs=(P("gx", "gy", "gz", None), P("gx", "gy", "gz", None), P(), P()),
        check_vma=False,
    )
```

profile of v0, /device:TPU:6, one launch (start us, length us, event | category | flops | bytes accessed | tf_op | source)
XLA Modules:
  0.0 44.1 jit_solution(11414187515732566133)
XLA Ops:
  0.6 0.7 %copy.12 = s32[1,2,2,6,32]{4,3,2,1,0:T(8,128)S(1)} copy(s32[1,2,2,6,32]{4,2,3,1,0:T(2,128)} %param.13) | data formatting | bytes 6144 | tf_op args[6]
  1.3 0.0 copy-start
  1.3 0.0 copy-start.1
  1.3 0.0 copy-start.2
  1.4 0.0 copy-start.3
  1.4 0.0 copy-start.4
  1.4 1.1 %reshape.32.params = f32[4,68,128]{2,1,0:T(8,128)S(1)} reshape(f32[1,2,2,8704]{3,2,1,0:T(2,128)} %param.7) | data formatting | bytes 278528 | tf_op jit(solution)/shard_map/reshape | solution.py:720
  2.4 0.0 copy-done
  2.5 0.0 copy-done.1
  2.5 0.0 copy-done.2
  2.5 0.0 copy-done.3
  2.5 0.0 copy-done.4
  2.5 39.1 %shard_map.102 = (f32[4,128]{1,0:T(4,128)S(1)}, f32[4,68,128]{2,1,0:T(8,128)S(1)}, f32[8,512]{1,0:T(8,128)S(1)}) custom-call(f32[4,68,128]{2,1,0:T(8,128)S(1)} %reshape.32.params, f32[5,512]{1,0:T(8,128)S(1)} %copy-done, f32[1,512]{1,0:T(1,128)S(1)} %bitcast.11, f32[4,4,128]{2,1,0:T(4,128)S(1)} %bitcast.10, f32[4,128]{1,0:T(4,128)S(1)} %bitcast.12, ...), custom_call_target="tpu_custom_call" | custom-call | tf_op jit(solution)/shard_map/pallas_call | solution.py:666
  41.6 0.6 %slice.7 = f32[1,512]{1,0:T(1,128)} slice(f32[8,512]{1,0:T(8,128)S(1)} %get-tuple-element.9), slice={[5:6], [0:512]} | slice | bytes 4096 | tf_op jit(solution)/shard_map/slice | solution.py:732
  42.2 0.7 %reshape.39 = f32[1,2,2,8704]{3,2,1,0:T(2,128)} reshape(f32[4,68,128]{2,1,0:T(8,128)S(1)} %get-tuple-element.8) | data formatting | bytes 278528 | tf_op jit(solution)/shard_map/reshape | solution.py:730
  42.9 0.6 %copy.15 = f32[1,2,2,128]{3,2,1,0:T(2,128)} copy(f32[1,2,2,128]{3,2,1,0:T(2,128)S(1)} %bitcast.13) | data formatting | bytes 4096
  43.5 0.6 %copy.16 = f32[5,512]{1,0:T(8,128)} copy(f32[5,512]{1,0:T(8,128)S(1)} %bitcast.9) | data formatting | bytes 20480
Async XLA Ops:
  1.3 1.1 %copy-start = (f32[5,512]{1,0:T(8,128)S(1)}, f32[5,512]{1,0:T(8,128)}, u32[]{:S(2)}) copy-start(f32[5,512]{1,0:T(8,128)} %inner.1) | copy-start | bytes 30724
  1.3 1.1 %copy-start.1 = (f32[1,2,2,4,128]{4,3,2,1,0:T(4,128)S(1)}, f32[1,2,2,4,128]{4,3,2,1,0:T(4,128)}, u32[]{:S(2)}) copy-start(f32[1,2,2,4,128]{4,3,2,1,0:T(4,128)} %param.10) | copy-start | bytes 24580
  1.3 1.1 %copy-start.2 = (f32[512]{0:T(512)S(1)}, f32[512]{0:T(512)}, u32[]{:S(2)}) copy-start(f32[512]{0:T(512)} %param.9) | copy-start | bytes 6148
  1.4 1.1 %copy-start.3 = (f32[1,2,2,128]{3,2,1,0:T(2,128)S(1)}, f32[1,2,2,128]{3,2,1,0:T(2,128)}, u32[]{:S(2)}) copy-start(f32[1,2,2,128]{3,2,1,0:T(2,128)} %param.11) | copy-start | bytes 6148
  1.4 1.1 %copy-start.4 = (f32[1,2,2]{2,1,0:T(2,128)S(1)}, f32[1,2,2]{2,1,0:T(2,128)}, u32[]{:S(2)}) copy-start(f32[1,2,2]{2,1,0:T(2,128)} %param.12) | copy-start | bytes 52
where the time goes:
time: 44.2 us; the launch traced here: 44.1 us
  Pallas kernels  39.1 us (88%)
  local copies, waits for them, and re-layouts  4.31 us (10%)
  between operations  0.7 us (2%)
    pallas_call x1, Pallas kernels, on_device(): pl.pallas_call(partial(kernel, sizes), out_shape=(jax.ShapeDtypeStruct((N...  39.1 us
    unnamed x13, local copies, waits for them, and re-layouts  1.92 us
    reshape x1, local copies, waits for them, and re-layouts, on_device(): fine_params.reshape(NETS, ROWS, PTS)  1.07 us

commit v1 on v0

--- a/solution.py
+++ b/solution.py
@@ -72,6 +72,22 @@
 
 def kernel(
     sizes,
+    params_hbm,
+    inner_hbm,
+    outer_hbm,
+    points_hbm,
+    source_hbm,
+    kappa_hbm,
+    faces_hbm,
+    res_far,
+    grad_far,
+    inner_far,
+    outer_far,
+    res_out,
+    grad_out,
+    inner_out,
+    outer_out,
+    out_sem,
     params,
     inner,
     outer,
@@ -79,9 +95,7 @@
     source,
     kappa,
     faces,
-    res_out,
-    grad_out,
-    coarse_out,
+    in_sem,
     hot,
     gbuf,
     gin,
@@ -99,7 +113,7 @@
     act2,
     hid1,
     state2,
-    dlast,
+    state3,
     qs,
     dz,
     acc3,
@@ -108,10 +122,10 @@
     acco,
     work,
     eown,
-    ecoarse,
     ccols,
     cact,
-    cvec,
+    cone,
+    csums,
     ar,
     g_send,
     g_recv,
@@ -121,21 +135,59 @@
     r_recv,
     ar_send,
     ar_recv,
+    tokens,
+    flat_out,
 ):
     place = [lax.axis_index(axis) for axis in AXES]
+    fetches = [
+        pltpu.make_async_copy(far, near, in_sem.at[k])
+        for k, (far, near) in enumerate(
+            (
+                (points_hbm, points),
+                (faces_hbm, faces),
+                (kappa_hbm, kappa),
+                (params_hbm, params),
+                (inner_hbm, inner),
+                (outer_hbm, outer),
+                (source_hbm, source),
+            )
+        )
+    ]
+    for fetch in fetches:
+        fetch.start()
 
     def target(slot, flip):
         axis = slot // 2
         sign = (2 * (slot % 2) - 1) * (-1 if flip else 1)
         return AXES[axis], place[axis] + sign, sizes[axis]
 
-    low = min(4, sizes[0])
     groups = [
-        ("gy", place[1], sizes[1], lambda p: p),
-        ("gz", place[2], sizes[2], lambda p: p),
-        ("gx", place[0] % low, low, lambda p: (place[0] // low) * low + p),
-        ("gx", place[0] // low, sizes[0] // low, lambda p: p * low + place[0] % low),
+        (
+            place[1] * sizes[2] + place[2],
+            sizes[1] * sizes[2],
+            lambda p: {"gy": p // sizes[2], "gz": lax.rem(p, sizes[2])},
+        ),
+        (place[0], sizes[0], lambda p: {"gx": p}),
     ]
+
+    def ring(axis, step):
+        return {AXES[axis]: lax.rem(place[axis] + step + sizes[axis], sizes[axis])}
+
+    def pass_on(level, axes):
+        for axis in axes:
+            reach = (1 << level) if axis == 0 else 1
+            for side in range(2):
+                pl.semaphore_signal(
+                    tokens.at[level, 2 * axis + side],
+                    inc=1,
+                    device_id=ring(axis, reach if side else -reach),
+                    device_id_type=MESH,
+                )
+
+    def hear(level, axes):
+        for axis in axes:
+            for side in range(2):
+                pl.semaphore_wait(tokens.at[level, 2 * axis + side], 1)
 
     def exchange(source_of, landing, send_sem, recv_sem, flip):
         for slot in range(6):
@@ -171,18 +223,18 @@
                 ).wait_send()
 
     def ar_copies(stage, arriving):
-        axis, pos, size, member = groups[stage]
+        pos, size, member = groups[stage]
         for k in range(1, size):
             partner = lax.rem(pos + k, size)
             slot = partner if arriving else pos
             yield pltpu.make_async_remote_copy(
                 ar.at[stage, pos], ar.at[stage, slot],
                 ar_send.at[stage, partner], ar_recv.at[stage, slot],
-                device_id={axis: member(partner)}, device_id_type=MESH,
+                device_id=member(partner), device_id_type=MESH,
             )
 
     def ar_start(stage, value):
-        ar[stage, groups[stage][1]] = value
+        ar[stage, groups[stage][0]] = value
         for out in ar_copies(stage, False):
             out.start()
 
@@ -190,7 +242,7 @@
         for back in ar_copies(stage, True):
             back.wait_recv()
         total = ar[stage, 0]
-        for p in range(1, groups[stage][2]):
+        for p in range(1, groups[stage][1]):
             total = total + ar[stage, p]
         return total
 
@@ -199,38 +251,26 @@
     rin[...] = jnp.zeros_like(rin)
 
     barrier = pltpu.get_barrier_semaphore()
-    expected = 0
-    for slot in (0, 1):
-        axis, where, size = target(slot, False)
-        present = jnp.logical_and(where >= 0, where < size)
-
-        @pl.when(present)
-        def _(axis=axis, where=where):
-            pl.semaphore_signal(barrier, inc=1, device_id={axis: where}, device_id_type=MESH)
-
-        expected = expected + jnp.where(present, 1, 0)
-    for axis, pos, size, member in groups:
-        for k in range(1, size):
-            pl.semaphore_signal(
-                barrier, inc=1, device_id={axis: member(lax.rem(pos + k, size))}, device_id_type=MESH
-            )
-        expected = expected + (size - 1)
+    for axis in range(3):
+        for step in (-1, 1):
+            pl.semaphore_signal(barrier, inc=1, device_id=ring(axis, step), device_id_type=MESH)
 
     lane = iota((1, PTS), 1)
     row8 = iota((8, PTS), 0)
     group = lane // FACE
+    for fetch in fetches[0:3]:
+        fetch.wait()
     for j in range(NETS):
         b, c = j // 2, j % 2
-        index = faces[j]
-        first = jnp.concatenate([index[k : k + 1] for k in range(4)], axis=1)
-        second = jnp.concatenate(
-            [index[4:5], index[5:6], jnp.full((1, 2 * FACE), -1, jnp.int32)], axis=1
-        )
+        index = [faces[b, k, c : c + 1, :] for k in range(6)]
+        first = jnp.concatenate(index[0:4], axis=1)
+        second = jnp.concatenate(index[4:6] + [jnp.full((1, 2 * FACE), -1, jnp.int32)], axis=1)
         point = iota((PTS, PTS), 0)
         hot[j, :, 0:PTS] = jnp.where(point == first, 1.0, 0.0).astype(BF)
         hot[j, :, PTS : 2 * PTS] = jnp.where(point == second, 1.0, 0.0).astype(BF)
         own = jnp.concatenate([points[j], jnp.zeros((4, PTS), F32)], axis=0)
-        own = jnp.where(row8 == 4, kappa[b, c], own)
+        own = jnp.where(row8 == 4, kappa[b : b + 1, c : c + 1], own)
+        own = jnp.where(row8 == 5, 1.0, own)
         xs[j, 0] = own
         hi, mid, low_part = split3(own)
         pieces = jnp.concatenate([hi, mid, low_part, jnp.zeros_like(hi)], axis=0)
@@ -241,13 +281,16 @@
         gbuf[0, j] = moved[:, 0:PTS] - shift_a
         gbuf[1, j] = moved[:, PTS : 2 * PTS] - shift_b
 
-    pl.semaphore_wait(barrier, expected)
+    pl.semaphore_wait(barrier, 6)
     g_args = (lambda slot: gbuf.at[slot // 4], gin, g_send, g_recv, False)
     exchange(*g_args)
-
+    pass_on(0, (0, 1, 2))
+
+    for fetch in fetches[3:]:
+        fetch.wait()
     half = iota((32, PTS), 1) < HID
     for n in range(NETS):
-        flat = params[n]
+        flat = params[n // 2, :, n % 2, :]
         even = pltpu.roll(jnp.where(half, flat[35:67], flat[2:34]), HID, 1)
         odd = jnp.where(half, flat[3:35], flat[35:67])
         work[pl.ds(0, 32, stride=2), :] = even
@@ -339,39 +382,49 @@
             z = [product[:, at - begin + k * PTS : at - begin + (k + 1) * PTS] for k in range(CH)]
             coef = coefficients(xs[n, tile])
             hidden = jnp.tanh(z[0] + wide[n, 6])
-            squared = hidden * hidden
-            one = 1.0 - squared
+            one = 1.0 - hidden * hidden
             two = -2.0 * hidden * one
-            three = -2.0 * one * (1.0 - 3.0 * squared)
             mixed = coef[5] * z[5]
             for k in range(1, 5):
                 mixed = mixed + coef[k] * z[k]
             curved = coef[5] * (z[1] * z[1] + z[2] * z[2] + z[3] * z[3])
             q = coef[0] * hidden + one * mixed + two * curved
+            state3[n, :, at : at + PTS] = hidden
+            for k in range(1, 4):
+                state3[n, :, at + k * PTS : at + (k + 1) * PTS] = z[k]
+            state3[n, :, at + 4 * PTS : at + 5 * PTS] = mixed
+            state3[n, :, at + 5 * PTS : at + 6 * PTS] = q
+            results.append(jnp.sum(wide[n, 7] * q, axis=0, keepdims=True))
+        return results
+
+    def backward(n, tiles, rows, add):
+        begin, end = tiles[0] * WIDTH, (tiles[-1] + 1) * WIDTH
+
+        def collect(ref, value):
+            ref[n] = ref[n] + value if add else value
+
+        for tile, row in zip(tiles, rows):
+            at = tile * WIDTH
+            coef = [value * row for value in coefficients(xs[n, tile])]
+            hidden, z1, z2, z3, mixed, q = (
+                state3[n, :, at + k * PTS : at + (k + 1) * PTS] for k in range(CH)
+            )
             hi, lo = split2(q)
             qs[n, 0:64, tile * PTS : (tile + 1) * PTS] = hi
             qs[n, 64:128, tile * PTS : (tile + 1) * PTS] = lo
+            squared = hidden * hidden
+            one = 1.0 - squared
+            three = -2.0 * one * (1.0 - 3.0 * squared)
             out = wide[n, 7]
-            results.append(jnp.sum(out * q, axis=0, keepdims=True))
-            one, two, three = out * one, out * two, out * three
+            one = out * one
+            two = -2.0 * hidden * one
+            curved = coef[5] * (z1 * z1 + z2 * z2 + z3 * z3)
+            put(dz, 0, at, coef[0] * one + two * (mixed * row) + (out * three) * curved)
             twice = 2.0 * coef[5] * two
-            dlast[n, :, at : at + PTS] = coef[0] * one + two * mixed + three * curved
-            for k in range(1, 4):
-                dlast[n, :, at + k * PTS : at + (k + 1) * PTS] = coef[k] * one + twice * z[k]
-            dlast[n, :, at + 4 * PTS : at + 5 * PTS] = coef[4] * one
-            dlast[n, :, at + 5 * PTS : at + 6 * PTS] = coef[5] * one
-        return results
-
-    def backward(n, tiles, rows, add):
-        begin, end = tiles[0] * WIDTH, (tiles[-1] + 1) * WIDTH
-
-        def collect(ref, value):
-            ref[n] = ref[n] + value if add else value
-
-        for tile, row in zip(tiles, rows):
-            for k in range(CH):
-                at = tile * WIDTH + k * PTS
-                put(dz, 0, at, dlast[n, :, at : at + PTS] * row)
+            for k, z in ((1, z1), (2, z2), (3, z3)):
+                put(dz, 0, at + k * PTS, coef[k] * one + twice * z)
+            put(dz, 0, at + 4 * PTS, coef[4] * one)
+            put(dz, 0, at + 5 * PTS, coef[5] * one)
         product = dot(lb[n, 1], dz[0, 0:192, begin:end])
         collect(acc3, dot_nt(act2[n, 64:208, begin:end], dz[0, 0:128, begin:end]))
         row = jnp.concatenate(rows, axis=1)
@@ -433,41 +486,6 @@
 
     lax.fori_loop(0, NETS, own_forward, 0)
 
-    arrive(*g_args)
-    def choose(parts):
-        picked = parts[-1]
-        for k in range(len(parts) - 2, -1, -1):
-            picked = jnp.where(group == k, parts[k], picked)
-        return picked
-
-    blank = jnp.zeros((8, PTS), F32)
-    for n in range(NETS):
-        b, c = n // 2, n % 2
-        slots = [
-            gin[0, n],
-            gin[1, n],
-            gbuf[0, n + 2] if b == 0 else gin[2, n - 2],
-            gbuf[0, n - 2] if b == 1 else gin[3, n + 2],
-        ]
-        xs[n, 1] = choose(slots)
-        slots = [
-            gbuf[1, n + 1] if c == 0 else gin[4, n - 1],
-            gbuf[1, n - 1] if c == 1 else gin[5, n + 1],
-            blank,
-        ]
-        xs[n, 2] = choose(slots)
-
-    def face_forward(n, carry):
-        first, second = forward(n, (1, 2))
-        ebuf[0, pl.ds(n, 1), :] = first
-        ebuf[1, pl.ds(n, 1), :] = second
-        return carry
-
-    ebuf[...] = jnp.zeros_like(ebuf)
-    lax.fori_loop(0, NETS, face_forward, 0)
-    e_args = (lambda slot: ebuf.at[slot // 4], ein, e_send, e_recv, True)
-    exchange(*e_args)
-
     scales = (2.0 / sizes[0], 2.0 / (2 * sizes[1]), 2.0 / (2 * sizes[2]))
     ci = inner[...]
     co = outer[...]
@@ -487,19 +505,20 @@
     ).T
     ccols[0] = jnp.broadcast_to(two_rows[:, 0:1], (COARSE, PTS))
     ccols[1] = jnp.broadcast_to(two_rows[:, 1:2], (COARSE, PTS))
-    for j in range(NETS):
-        b, c = j // 2, j % 2
+
+    def coarse_inputs(n, x):
+        b, c = n // 2, n % 2
         centres = (
             place[0].astype(F32) + 0.5,
             (2 * place[1] + b).astype(F32) + 0.5,
             (2 * place[2] + c).astype(F32) + 0.5,
         )
-        own = xs[j, 0]
-        v = jnp.where(row8 == 3, own, 0.0)
+        v = jnp.where(row8 == 3, x, 0.0)
         for k in range(3):
-            v = jnp.where(row8 == k, (centres[k] + own) * scales[k] - 1.0, v)
-        v = jnp.where(row8 == 4, 1.0, v)
-        cvec[j] = v
+            v = jnp.where(row8 == k, (centres[k] + x) * scales[k] - 1.0, v)
+        return jnp.where(row8 == 4, 1.0, v)
+
+    def coarse_forward(block, v, wanted):
         hi = v.astype(BF).astype(F32)
         mid = (v - hi).astype(BF).astype(F32)
         lo = v - hi - mid
@@ -509,13 +528,133 @@
         one = 1.0 - squared
         curve = one * hidden
         bend = one * (1.0 - 3.0 * squared)
-        ecoarse[j : j + 1, :] = jnp.sum(
-            ccols[0] * one + ccols[1] * (curve * kappa[b, c]), axis=0, keepdims=True
+        cone[:, block * PTS : (block + 1) * PTS] = one
+        for k, value in enumerate((curve, bend)):
+            hi, lo = split2(value)
+            cact[2 * k, :, block * PTS : (block + 1) * PTS] = hi
+            cact[2 * k + 1, :, block * PTS : (block + 1) * PTS] = lo
+        if wanted is not None:
+            return jnp.sum(
+                ccols[0] * one + ccols[1] * (curve * wanted), axis=0, keepdims=True
+            )
+
+    def coarse_sums(blocks, first):
+        lefts = []
+        for weight, v, conductivity in blocks:
+            plain = weight * v
+            plain = jnp.concatenate([plain, plain * conductivity], axis=0)
+            hi = plain.astype(BF).astype(F32)
+            lefts.append(jnp.concatenate([hi, plain - hi], axis=0))
+        left = jnp.concatenate(lefts, axis=1).astype(BF)
+        span = slice(first * PTS, (first + len(blocks)) * PTS)
+        sums = []
+        for k in range(2):
+            upper = dot_nt(left, cact[2 * k, :, span])
+            lower = dot_nt(left, cact[2 * k + 1, :, span])
+            sums.append(upper[0:16] + upper[16:32] + lower[0:16])
+        weighted = None
+        for k, (weight, _, _) in enumerate(blocks):
+            term = cone[:, (first + k) * PTS : (first + k + 1) * PTS] * weight
+            weighted = term if weighted is None else weighted + term
+        hi, lo = split2(weighted)
+        ones = jnp.ones((16, PTS), BF)
+        sums.append(dot_nt(ones, hi) + dot_nt(ones, lo))
+        return sums
+
+    blocks = []
+    for j in range(NETS):
+        x = xs[j, 0]
+        v = coarse_inputs(j, x)
+        base = eown[j, 0:1, :] + coarse_forward(j, v, x[4:5]) - source[j : j + 1, :]
+        eown[j, 0:1, :] = base
+        blocks.append((base * (1.0 / PTS), v, x[4:5]))
+    own_sums = coarse_sums(blocks, 0)
+    for k in range(3):
+        csums[k] = own_sums[k]
+
+    hear(0, (0, 1, 2))
+    pass_on(1, (0, 1, 2))
+
+    arrive(*g_args)
+    def choose(parts):
+        picked = parts[-1]
+        for k in range(len(parts) - 2, -1, -1):
+            picked = jnp.where(group == k, parts[k], picked)
+        return picked
+
+    blank = jnp.zeros((8, PTS), F32)
+    for n in range(NETS):
+        b, c = n // 2, n % 2
+        slots = [
+            gin[0, n],
+            gin[1, n],
+            gbuf[0, n + 2] if b == 0 else gin[2, n - 2],
+            gbuf[0, n - 2] if b == 1 else gin[3, n + 2],
+        ]
+        xs[n, 1] = choose(slots)
+        slots = [
+            gbuf[1, n + 1] if c == 0 else gin[4, n - 1],
+            gbuf[1, n - 1] if c == 1 else gin[5, n + 1],
+            blank,
+        ]
+        xs[n, 2] = choose(slots)
+
+    def face_forward(n, carry):
+        first, second = forward(n, (1, 2))
+        ebuf[0, pl.ds(n, 1), :] = first
+        ebuf[1, pl.ds(n, 1), :] = second
+        return carry
+
+    ebuf[...] = jnp.zeros_like(ebuf)
+    lax.fori_loop(0, 2, face_forward, 0)
+    hear(1, (1, 2))
+    pass_on(2, (1, 2))
+    lax.fori_loop(2, NETS, face_forward, 0)
+    e_args = (lambda slot: ebuf.at[slot // 4], ein, e_send, e_recv, True)
+    exchange(*e_args)
+
+    hear(1, (0,))
+    pass_on(2, (0,))
+    def joined_halves(first, second):
+        return jnp.where(lane < HID, first, pltpu.roll(second, HID, 1))
+
+    weights, inputs, levels = [], [], []
+    for n in range(NETS):
+        for tile in range(2):
+            x = xs[n, tile + 1]
+            weights.append(ebuf[tile, n : n + 1, :] * x[5:6] * (1.0 / PTS))
+            inputs.append(coarse_inputs(n, x))
+            levels.append(x[4:5])
+    blocks = [(weights[2 * n], inputs[2 * n], levels[2 * n]) for n in range(NETS)]
+    for n in range(0, NETS, 2):
+        blocks.append(
+            tuple(
+                joined_halves(values[2 * n + 1], values[2 * n + 3])
+                for values in (weights, inputs, levels)
+            )
         )
-        for k, value in enumerate((curve, bend, one)):
-            hi, lo = split2(value)
-            cact[2 * k, :, j * PTS : (j + 1) * PTS] = hi
-            cact[2 * k + 1, :, j * PTS : (j + 1) * PTS] = lo
+    for k, (_, v, _) in enumerate(blocks):
+        coarse_forward(NETS + k, v, None)
+    sums = [csums[k] + part for k, part in enumerate(coarse_sums(blocks, NETS))]
+    s_one, s_curve = sums[2][0:1], sums[0][12:13]
+    moments = co * (2.0 * squares * sums[1][8:13] - 4.0 * ci[3:4] * sums[0][0:5])
+    extra = jnp.concatenate(
+        [
+            (4.0 * scales[0] * scales[0]) * ci[0:1] * co * s_curve,
+            (4.0 * scales[1] * scales[1]) * ci[1:2] * co * s_curve,
+            (4.0 * scales[2] * scales[2]) * ci[2:3] * co * s_curve,
+            2.0 * co * s_one,
+            jnp.zeros((1, COARSE), F32),
+        ],
+        axis=0,
+    )
+    outer_grad = 2.0 * ci[3:4] * s_one + 2.0 * squares * s_curve
+    partial_sums = jnp.concatenate([moments + extra, outer_grad], axis=0)
+    hear(2, (1, 2))
+    ar_start(
+        0,
+        jnp.concatenate([partial_sums[:, k * PTS : (k + 1) * PTS] for k in range(4)], axis=0),
+    )
 
     arrive(*e_args)
     for j in range(NETS):
@@ -540,8 +679,7 @@
             ]
         )
         spread = dot_nt(stacked3(jnp.concatenate([first, second], axis=1)), hot[j])
-        fine = eown[j, 0:1, :] + spread[0:1] + spread[1:2] + spread[2:3]
-        residual = fine + ecoarse[j : j + 1, :] - source[j : j + 1, :]
+        residual = eown[j, 0:1, :] + spread[0:1] + spread[1:2] + spread[2:3]
         res_out[j : j + 1, :] = residual
         scaled = residual * (1.0 / PTS)
         eown[j] = jnp.broadcast_to(scaled, (8, PTS))
@@ -553,45 +691,13 @@
     r_args = (lambda slot: rbuf.at[slot // 4], rin, r_send, r_recv, False)
     exchange(*r_args)
 
-    blocks = []
-    for j in range(NETS):
-        b, c = j // 2, j % 2
-        plain = eown[j] * cvec[j]
-        plain = jnp.concatenate([plain, plain * kappa[b, c]], axis=0)
-        hi = plain.astype(BF).astype(F32)
-        blocks.append(jnp.concatenate([hi, plain - hi], axis=0))
-    left = jnp.concatenate(blocks, axis=1).astype(BF)
-    sums = []
-    for k in range(3):
-        upper = dot_nt(left, cact[2 * k])
-        lower = dot_nt(left, cact[2 * k + 1])
-        sums.append(upper[0:16] + upper[16:32] + lower[0:16])
-    s_one, s_curve = sums[2][4:5], sums[0][12:13]
-    moments = co * (2.0 * squares * sums[1][8:13] - 4.0 * ci[3:4] * sums[0][0:5])
-    extra = jnp.concatenate(
-        [
-            (4.0 * scales[0] * scales[0]) * ci[0:1] * co * s_curve,
-            (4.0 * scales[1] * scales[1]) * ci[1:2] * co * s_curve,
-            (4.0 * scales[2] * scales[2]) * ci[2:3] * co * s_curve,
-            2.0 * co * s_one,
-            jnp.zeros((1, COARSE), F32),
-        ],
-        axis=0,
-    )
-    outer_grad = 2.0 * ci[3:4] * s_one + 2.0 * squares * s_curve
-    partial_sums = jnp.concatenate(
-        [moments + extra, outer_grad, jnp.zeros((2, COARSE), F32)], axis=0
-    )
-    ar_start(0, partial_sums)
-
     def own_backward(n, carry):
         backward(n, (0,), [eown[n, 0:1, :]], False)
         return carry
 
-    lax.fori_loop(0, 2, own_backward, 0)
+    lax.fori_loop(0, NETS, own_backward, 0)
+    hear(2, (0,))
     ar_start(1, ar_finish(0))
-    lax.fori_loop(2, NETS, own_backward, 0)
-    ar_start(2, ar_finish(1))
 
     arrive(*r_args)
     for n in range(NETS):
@@ -632,47 +738,84 @@
         first = first[:, 0:64] + first[:, 64:128]
         last = acco[n, 0:1, :] + acco[n, 1:2, :] + acco[n, 2:3, :]
         last = last[:, 0:64] + last[:, 64:128]
-        grad_out[n, 0:1, 0:64] = first[0:1]
-        grad_out[n, 0:1, 64:128] = first[1:2]
-        grad_out[n, 1:2, 0:64] = first[2:3]
-        grad_out[n, 1:2, 64:128] = first[3:4]
-        grad_out[n, 2:3, 0:64] = first[4:5]
-        grad_out[n, 2:34, 64:128] = even[:, 0:64]
-        grad_out[n, 3:35, 0:64] = odd[:, 0:64]
-        grad_out[n, 34:35, 64:128] = bias2
-        grad_out[n, 35:67, 0:64] = even[:, 64:128]
-        grad_out[n, 35:67, 64:128] = odd[:, 64:128]
-        grad_out[n, 67:68, 0:64] = bias3
-        grad_out[n, 67:68, 64:128] = last
+        flat_out[n, 0:1, 0:64] = first[0:1]
+        flat_out[n, 0:1, 64:128] = first[1:2]
+        flat_out[n, 1:2, 0:64] = first[2:3]
+        flat_out[n, 1:2, 64:128] = first[3:4]
+        flat_out[n, 2:3, 0:64] = first[4:5]
+        flat_out[n, 2:34, 64:128] = even[:, 0:64]
+        flat_out[n, 3:35, 0:64] = odd[:, 0:64]
+        flat_out[n, 34:35, 64:128] = bias2
+        flat_out[n, 35:67, 0:64] = even[:, 64:128]
+        flat_out[n, 35:67, 64:128] = odd[:, 64:128]
+        flat_out[n, 67:68, 0:64] = bias3
+        flat_out[n, 67:68, 64:128] = last
         return carry
 
-    lax.fori_loop(0, 2, face_backward, 0)
-    ar_start(3, ar_finish(2))
-    lax.fori_loop(2, NETS, face_backward, 0)
+    lax.fori_loop(0, NETS, face_backward, 0)
     count = NETS * sizes[0] * sizes[1] * sizes[2]
-    coarse_out[...] = ar_finish(3) * (count ** (-0.5))
-
+    for n in range(NETS):
+        grad_out[n // 2, :, n % 2, :] = flat_out[n]
+    stores = [
+        pltpu.make_async_copy(near, away, out_sem.at[k])
+        for k, (near, away) in enumerate(
+            (
+                (res_out, res_far),
+                (grad_out, grad_far),
+                (inner_out, inner_far),
+                (outer_out, outer_far),
+            )
+        )
+    ]
+    stores[0].start()
+    stores[1].start()
     for args in (g_args, e_args, r_args):
         sent(*args)
-    for stage in range(4):
+    total = ar_finish(1) * (count ** (-0.5))
+    for k in range(4):
+        inner_out[:, k * PTS : (k + 1) * PTS] = total[6 * k : 6 * k + 5]
+        outer_out[:, k * PTS : (k + 1) * PTS] = total[6 * k + 5 : 6 * k + 6]
+    stores[2].start()
+    stores[3].start()
+    for store in stores:
+        store.wait()
+    for stage in range(2):
         for out in ar_copies(stage, False):
             out.wait_send()
 
 
+def writer(*refs):
+    for k in range(4):
+        refs[k + 4][...] = refs[k][...]
+
+
 def on_device(fine_params, coarse_inner, coarse_outer, points, source, conductivity, face_points):
     sizes = tuple(lax.axis_size(axis) for axis in AXES)
-    vmem = pl.BlockSpec(memory_space=pltpu.VMEM)
-    smem = pl.BlockSpec(memory_space=pltpu.SMEM)
-    residual, grads, coarse = pl.pallas_call(
+    far = pl.BlockSpec(memory_space=pltpu.HBM)
+    results = pl.pallas_call(
         partial(kernel, sizes),
         out_shape=(
             jax.ShapeDtypeStruct((NETS, PTS), F32),
-            jax.ShapeDtypeStruct((NETS, ROWS, PTS), F32),
-            jax.ShapeDtypeStruct((8, COARSE), F32),
+            jax.ShapeDtypeStruct((2, ROWS, 2, PTS), F32),
+            jax.ShapeDtypeStruct((5, COARSE), F32),
+            jax.ShapeDtypeStruct((1, COARSE), F32),
         ),
-        in_specs=[vmem, vmem, vmem, vmem, vmem, smem, vmem],
-        out_specs=(vmem, vmem, vmem),
+        in_specs=[far] * 7,
+        out_specs=(far,) * 4,
         scratch_shapes=[
+            pltpu.VMEM((NETS, PTS), F32),
+            pltpu.VMEM((2, ROWS, 2, PTS), F32),
+            pltpu.VMEM((5, COARSE), F32),
+            pltpu.VMEM((1, COARSE), F32),
+            pltpu.SemaphoreType.DMA((4,)),
+            pltpu.VMEM((2, ROWS, 2, PTS), F32),
+            pltpu.VMEM((5, COARSE), F32),
+            pltpu.VMEM((1, COARSE), F32),
+            pltpu.VMEM((NETS, 4, PTS), F32),
+            pltpu.VMEM((NETS, PTS), F32),
+            pltpu.VMEM((2, 2), F32),
+            pltpu.VMEM((2, 6, 2, FACE), jnp.int32),
+            pltpu.SemaphoreType.DMA((7,)),
             pltpu.VMEM((NETS, PTS, 2 * PTS), BF),
             pltpu.VMEM((2, NETS, 8, PTS), F32),
             pltpu.VMEM((6, NETS, 8, PTS), F32),
@@ -699,37 +842,46 @@
             pltpu.VMEM((NETS, 16, PTS), F32),
             pltpu.VMEM((HID, PTS), F32),
             pltpu.VMEM((NETS, 8, PTS), F32),
-            pltpu.VMEM((8, PTS), F32),
             pltpu.VMEM((2, COARSE, PTS), F32),
-            pltpu.VMEM((6, COARSE, NETS * PTS), BF),
-            pltpu.VMEM((NETS, 8, PTS), F32),
-            pltpu.VMEM((4, 4, 8, COARSE), F32),
+            pltpu.VMEM((4, COARSE, 10 * PTS), BF),
+            pltpu.VMEM((COARSE, 10 * PTS), F32),
+            pltpu.VMEM((3, 16, COARSE), F32),
+            pltpu.VMEM((2, 16, 24, PTS), F32),
             pltpu.SemaphoreType.DMA((6,)),
             pltpu.SemaphoreType.DMA((6,)),
             pltpu.SemaphoreType.DMA((6,)),
             pltpu.SemaphoreType.DMA((6,)),
             pltpu.SemaphoreType.DMA((6,)),
             pltpu.SemaphoreType.DMA((6,)),
-            pltpu.SemaphoreType.DMA((4, 4)),
-            pltpu.SemaphoreType.DMA((4, 4)),
+            pltpu.SemaphoreType.DMA((2, 16)),
+            pltpu.SemaphoreType.DMA((2, 16)),
+            pltpu.SemaphoreType.REGULAR((3, 6)),
+            pltpu.VMEM((NETS, ROWS, PTS), F32),
         ],
         compiler_params=pltpu.CompilerParams(
-            collective_id=0, has_side_effects=True, vmem_limit_bytes=48 * 1024 * 1024
+            collective_id=0, has_side_effects=True, vmem_limit_bytes=63 * 1024 * 1024
         ),
     )(
-        fine_params.reshape(NETS, ROWS, PTS),
+        fine_params.reshape(2, 2, ROWS, PTS).transpose(0, 2, 1, 3),
         coarse_inner,
         coarse_outer.reshape(1, COARSE),
         points.reshape(NETS, 4, PTS),
         source.reshape(NETS, PTS),
         conductivity.reshape(2, 2),
-        face_points.reshape(NETS, 6, FACE),
+        face_points.transpose(0, 1, 3, 2, 4).reshape(2, 6, 2, FACE),
     )
+    residual, grads, inner_grads, outer_grads = pl.pallas_call(
+        writer,
+        out_shape=tuple(jax.ShapeDtypeStruct(value.shape, F32) for value in results),
+        in_specs=[pl.BlockSpec(memory_space=pltpu.VMEM)] * 4,
+        out_specs=(pl.BlockSpec(memory_space=pltpu.VMEM),) * 4,
+        compiler_params=pltpu.CompilerParams(vmem_limit_bytes=63 * 1024 * 1024),
+    )(*results)
     return (
         residual.reshape(source.shape),
-        grads.reshape(fine_params.shape),
-        coarse[0:5],
-        coarse[5],
+        grads.transpose(0, 2, 1, 3).reshape(fine_params.shape),
+        inner_grads,
+        outer_grads.reshape(COARSE),
     )
 
 

time: 44.2 us -> 35.6 us (0.81)
  the two profiles are of different devices: /device:TPU:6 before, /device:TPU:1 now
where the time goes in v1:
time: 35.6 us; the launch traced here: 35.4 us
  Pallas kernels  34.8 us (98%)
  between operations  0.64 us (2%)
    pallas_call x1, Pallas kernels, on_device(): pl.pallas_call(partial(kernel, sizes), out_shape=(jax.ShapeDtypeStruct((N...  33.2 us
    pallas_call x1, Pallas kernels, on_device(): pl.pallas_call(writer, out_shape=tuple((jax.ShapeDtypeStruct(value.shape,...  1.58 us

profile of v1, /device:TPU:1, one launch (start us, length us, event | category | flops | bytes accessed | tf_op | source)
XLA Modules:
  0.0 35.4 jit_solution(5886943621562796562)
XLA Ops:
  0.6 33.2 %shard_map.102 = (f32[4,128]{1,0:T(4,128)}, f32[2,68,2,128]{3,2,1,0:T(2,128)}, f32[5,512]{1,0:T(8,128)}, f32[1,512]{1,0:T(1,128)}) custom-call(f32[2,68,2,128]{3,2,1,0:T(2,128)} %bitcast.15, f32[5,512]{1,0:T(8,128)} %inner_hbm.1, f32[1,512]{1,0:T(1,128)} %bitcast.18, f32[4,4,128]{2,1,0:T(4,128)} %bitcast.17, f32[4,128]{1,0:T(4,128)} %bitcast.19, ...), custom_call_target="tpu_custom_call" | custom-call | tf_op jit(solution)/shard_map/pallas_call | solution.py:795
  33.8 1.6 %shard_map.103 = (f32[4,128]{1,0:T(4,128)}, f32[2,68,2,128]{3,2,1,0:T(2,128)}, f32[5,512]{1,0:T(8,128)}, f32[1,512]{1,0:T(1,128)}) custom-call(f32[4,128]{1,0:T(4,128)} %get-tuple-element.12.refs_0_, f32[2,68,2,128]{3,2,1,0:T(2,128)} %get-tuple-element.13.refs_1_, f32[5,512]{1,0:T(8,128)} %get-tuple-element.14.refs_2_, f32[1,512]{1,0:T(1,128)} %get-tuple-element.15.refs_3_), custom_call_target="tpu_custom_call" | custom-call | tf_op jit(solution)/shard_map/pallas_call | solution.py:873

commit v2 on v1

--- a/solution.py
+++ b/solution.py
@@ -125,6 +125,7 @@
     ccols,
     cact,
     cone,
+    ccurve,
     csums,
     ar,
     g_send,
@@ -139,6 +140,105 @@
     flat_out,
 ):
     place = [lax.axis_index(axis) for axis in AXES]
+    def target(slot, flip):
+        axis = slot // 2
+        sign = (2 * (slot % 2) - 1) * (-1 if flip else 1)
+        return AXES[axis], place[axis] + sign, sizes[axis]
+
+    groups = [
+        (
+            place[1] * sizes[2] + place[2],
+            sizes[1] * sizes[2],
+            lambda p: {"gy": p // sizes[2], "gz": lax.rem(p, sizes[2])},
+        ),
+        (place[0], sizes[0], lambda p: {"gx": p}),
+    ]
+
+    def ring(axis, step):
+        return {AXES[axis]: lax.rem(place[axis] + step + sizes[axis], sizes[axis])}
+
+    def pass_on(level, axes):
+        for axis in axes:
+            reach = (1 << level) if axis == 0 else 1
+            for side in range(2):
+                pl.semaphore_signal(
+                    tokens.at[level, 2 * axis + side],
+                    inc=1,
+                    device_id=ring(axis, reach if side else -reach),
+                    device_id_type=MESH,
+                )
+
+    def hear(level, axes):
+        for axis in axes:
+            for side in range(2):
+                pl.semaphore_wait(tokens.at[level, 2 * axis + side], 1)
+
+    def exchange(source_of, landing, send_sem, recv_sem, flip):
+        for slot in range(6):
+            axis, where, size = target(slot, flip)
+
+            @pl.when(jnp.logical_and(where >= 0, where < size))
+            def _(slot=slot, axis=axis, where=where):
+                pltpu.make_async_remote_copy(
+                    source_of(slot), landing.at[slot], send_sem.at[slot], recv_sem.at[slot],
+                    device_id={axis: where}, device_id_type=MESH,
+                ).start()
+
+    def arrive(source_of, landing, send_sem, recv_sem, flip):
+        for slot in range(6):
+            axis, where, size = target(slot, not flip)
+
+            @pl.when(jnp.logical_and(where >= 0, where < size))
+            def _(slot=slot, axis=axis, where=where):
+                pltpu.make_async_remote_copy(
+                    source_of(slot), landing.at[slot], send_sem.at[slot], recv_sem.at[slot],
+                    device_id={axis: where}, device_id_type=MESH,
+                ).wait_recv()
+
+    def sent(source_of, landing, send_sem, recv_sem, flip):
+        for slot in range(6):
+            axis, where, size = target(slot, flip)
+
+            @pl.when(jnp.logical_and(where >= 0, where < size))
+            def _(slot=slot, axis=axis, where=where):
+                pltpu.make_async_remote_copy(
+                    source_of(slot), landing.at[slot], send_sem.at[slot], recv_sem.at[slot],
+                    device_id={axis: where}, device_id_type=MESH,
+                ).wait_send()
+
+    def ar_copies(stage, arriving):
+        pos, size, member = groups[stage]
+        for k in range(1, size):
+            partner = lax.rem(pos + k, size)
+            slot = partner if arriving else pos
+            yield pltpu.make_async_remote_copy(
+                ar.at[stage, pos], ar.at[stage, slot],
+                ar_send.at[stage, partner], ar_recv.at[stage, slot],
+                device_id=member(partner), device_id_type=MESH,
+            )
+
+    def ar_start(stage, value):
+        ar[stage, groups[stage][0]] = value
+        for out in ar_copies(stage, False):
+            out.start()
+
+    def ar_finish(stage):
+        for back in ar_copies(stage, True):
+            back.wait_recv()
+        total = ar[stage, 0]
+        for p in range(1, groups[stage][1]):
+            total = total + ar[stage, p]
+        return total
+
+    gin[...] = jnp.zeros_like(gin)
+    ein[...] = jnp.zeros_like(ein)
+    rin[...] = jnp.zeros_like(rin)
+
+    barrier = pltpu.get_barrier_semaphore()
+    for axis in range(3):
+        for step in (-1, 1):
+            pl.semaphore_signal(barrier, inc=1, device_id=ring(axis, step), device_id_type=MESH)
+
     fetches = [
         pltpu.make_async_copy(far, near, in_sem.at[k])
         for k, (far, near) in enumerate(
@@ -155,105 +255,6 @@
     ]
     for fetch in fetches:
         fetch.start()
-
-    def target(slot, flip):
-        axis = slot // 2
-        sign = (2 * (slot % 2) - 1) * (-1 if flip else 1)
-        return AXES[axis], place[axis] + sign, sizes[axis]
-
-    groups = [
-        (
-            place[1] * sizes[2] + place[2],
-            sizes[1] * sizes[2],
-            lambda p: {"gy": p // sizes[2], "gz": lax.rem(p, sizes[2])},
-        ),
-        (place[0], sizes[0], lambda p: {"gx": p}),
-    ]
-
-    def ring(axis, step):
-        return {AXES[axis]: lax.rem(place[axis] + step + sizes[axis], sizes[axis])}
-
-    def pass_on(level, axes):
-        for axis in axes:
-            reach = (1 << level) if axis == 0 else 1
-            for side in range(2):
-                pl.semaphore_signal(
-                    tokens.at[level, 2 * axis + side],
-                    inc=1,
-                    device_id=ring(axis, reach if side else -reach),
-                    device_id_type=MESH,
-                )
-
-    def hear(level, axes):
-        for axis in axes:
-            for side in range(2):
-                pl.semaphore_wait(tokens.at[level, 2 * axis + side], 1)
-
-    def exchange(source_of, landing, send_sem, recv_sem, flip):
-        for slot in range(6):
-            axis, where, size = target(slot, flip)
-
-            @pl.when(jnp.logical_and(where >= 0, where < size))
-            def _(slot=slot, axis=axis, where=where):
-                pltpu.make_async_remote_copy(
-                    source_of(slot), landing.at[slot], send_sem.at[slot], recv_sem.at[slot],
-                    device_id={axis: where}, device_id_type=MESH,
-                ).start()
-
-    def arrive(source_of, landing, send_sem, recv_sem, flip):
-        for slot in range(6):
-            axis, where, size = target(slot, not flip)
-
-            @pl.when(jnp.logical_and(where >= 0, where < size))
-            def _(slot=slot, axis=axis, where=where):
-                pltpu.make_async_remote_copy(
-                    source_of(slot), landing.at[slot], send_sem.at[slot], recv_sem.at[slot],
-                    device_id={axis: where}, device_id_type=MESH,
-                ).wait_recv()
-
-    def sent(source_of, landing, send_sem, recv_sem, flip):
-        for slot in range(6):
-            axis, where, size = target(slot, flip)
-
-            @pl.when(jnp.logical_and(where >= 0, where < size))
-            def _(slot=slot, axis=axis, where=where):
-                pltpu.make_async_remote_copy(
-                    source_of(slot), landing.at[slot], send_sem.at[slot], recv_sem.at[slot],
-                    device_id={axis: where}, device_id_type=MESH,
-                ).wait_send()
-
-    def ar_copies(stage, arriving):
-        pos, size, member = groups[stage]
-        for k in range(1, size):
-            partner = lax.rem(pos + k, size)
-            slot = partner if arriving else pos
-            yield pltpu.make_async_remote_copy(
-                ar.at[stage, pos], ar.at[stage, slot],
-                ar_send.at[stage, partner], ar_recv.at[stage, slot],
-                device_id=member(partner), device_id_type=MESH,
-            )
-
-    def ar_start(stage, value):
-        ar[stage, groups[stage][0]] = value
-        for out in ar_copies(stage, False):
-            out.start()
-
-    def ar_finish(stage):
-        for back in ar_copies(stage, True):
-            back.wait_recv()
-        total = ar[stage, 0]
-        for p in range(1, groups[stage][1]):
-            total = total + ar[stage, p]
-        return total
-
-    gin[...] = jnp.zeros_like(gin)
-    ein[...] = jnp.zeros_like(ein)
-    rin[...] = jnp.zeros_like(rin)
-
-    barrier = pltpu.get_barrier_semaphore()
-    for axis in range(3):
-        for step in (-1, 1):
-            pl.semaphore_signal(barrier, inc=1, device_id=ring(axis, step), device_id_type=MESH)
 
     lane = iota((1, PTS), 1)
     row8 = iota((8, PTS), 0)
@@ -484,7 +485,7 @@
         eown[n] = jnp.broadcast_to(forward(n, (0,))[0], (8, PTS))
         return carry
 
-    lax.fori_loop(0, NETS, own_forward, 0)
+    lax.fori_loop(0, NETS, own_forward, 0, unroll=4)
 
     scales = (2.0 / sizes[0], 2.0 / (2 * sizes[1]), 2.0 / (2 * sizes[2]))
     ci = inner[...]
@@ -505,6 +506,7 @@
     ).T
     ccols[0] = jnp.broadcast_to(two_rows[:, 0:1], (COARSE, PTS))
     ccols[1] = jnp.broadcast_to(two_rows[:, 1:2], (COARSE, PTS))
+    ccols[2] = 2.0 * ccols[0]
 
     def coarse_inputs(n, x):
         b, c = n // 2, n % 2
@@ -518,7 +520,7 @@
             v = jnp.where(row8 == k, (centres[k] + x) * scales[k] - 1.0, v)
         return jnp.where(row8 == 4, 1.0, v)
 
-    def coarse_forward(block, v, wanted):
+    def coarse_forward(block, v, conductivity, wanted):
         hi = v.astype(BF).astype(F32)
         mid = (v - hi).astype(BF).astype(F32)
         lo = v - hi - mid
@@ -527,45 +529,44 @@
         squared = hidden * hidden
         one = 1.0 - squared
         curve = one * hidden
-        bend = one * (1.0 - 3.0 * squared)
-        cone[:, block * PTS : (block + 1) * PTS] = one
-        for k, value in enumerate((curve, bend)):
-            hi, lo = split2(value)
-            cact[2 * k, :, block * PTS : (block + 1) * PTS] = hi
-            cact[2 * k + 1, :, block * PTS : (block + 1) * PTS] = lo
-        if wanted is not None:
-            return jnp.sum(
-                ccols[0] * one + ccols[1] * (curve * wanted), axis=0, keepdims=True
-            )
+        level = ccols[1] * conductivity
+        slope = level * (one * (1.0 - 3.0 * squared)) - ccols[2] * curve
+        at = slice(block * PTS, (block + 1) * PTS)
+        cone[:, at] = one
+        ccurve[:, at] = curve
+        hi, lo = split2(slope)
+        cact[0, :, at] = hi
+        cact[1, :, at] = lo
+        if wanted:
+            return jnp.sum(ccols[0] * one + level * curve, axis=0, keepdims=True)
 
     def coarse_sums(blocks, first):
         lefts = []
-        for weight, v, conductivity in blocks:
+        for weight, v, _ in blocks:
             plain = weight * v
-            plain = jnp.concatenate([plain, plain * conductivity], axis=0)
             hi = plain.astype(BF).astype(F32)
             lefts.append(jnp.concatenate([hi, plain - hi], axis=0))
         left = jnp.concatenate(lefts, axis=1).astype(BF)
         span = slice(first * PTS, (first + len(blocks)) * PTS)
-        sums = []
-        for k in range(2):
-            upper = dot_nt(left, cact[2 * k, :, span])
-            lower = dot_nt(left, cact[2 * k + 1, :, span])
-            sums.append(upper[0:16] + upper[16:32] + lower[0:16])
-        weighted = None
-        for k, (weight, _, _) in enumerate(blocks):
-            term = cone[:, (first + k) * PTS : (first + k + 1) * PTS] * weight
-            weighted = term if weighted is None else weighted + term
-        hi, lo = split2(weighted)
+        upper = dot_nt(left, cact[0, :, span])
+        lower = dot_nt(left, cact[1, :, span])
+        sums = [upper[0:8] + upper[8:16] + lower[0:8]]
         ones = jnp.ones((16, PTS), BF)
-        sums.append(dot_nt(ones, hi) + dot_nt(ones, lo))
+        for ref, powers in ((cone, 0), (ccurve, 1)):
+            weighted = None
+            for k, (weight, _, conductivity) in enumerate(blocks):
+                factor = weight * conductivity if powers else weight
+                term = ref[:, (first + k) * PTS : (first + k + 1) * PTS] * factor
+                weighted = term if weighted is None else weighted + term
+            hi, lo = split2(weighted)
+            sums.append((dot_nt(ones, hi) + dot_nt(ones, lo))[0:8])
         return sums
 
     blocks = []
     for j in range(NETS):
         x = xs[j, 0]
         v = coarse_inputs(j, x)
-        base = eown[j, 0:1, :] + coarse_forward(j, v, x[4:5]) - source[j : j + 1, :]
+        base = eown[j, 0:1, :] + coarse_forward(j, v, x[4:5], True) - source[j : j + 1, :]
         eown[j, 0:1, :] = base
         blocks.append((base * (1.0 / PTS), v, x[4:5]))
     own_sums = coarse_sums(blocks, 0)
@@ -606,10 +607,10 @@
         return carry
 
     ebuf[...] = jnp.zeros_like(ebuf)
-    lax.fori_loop(0, 2, face_forward, 0)
+    lax.fori_loop(0, 2, face_forward, 0, unroll=2)
     hear(1, (1, 2))
     pass_on(2, (1, 2))
-    lax.fori_loop(2, NETS, face_forward, 0)
+    lax.fori_loop(2, NETS, face_forward, 0, unroll=2)
     e_args = (lambda slot: ebuf.at[slot // 4], ein, e_send, e_recv, True)
     exchange(*e_args)
 
@@ -633,11 +634,10 @@
                 for values in (weights, inputs, levels)
             )
         )
-    for k, (_, v, _) in enumerate(blocks):
-        coarse_forward(NETS + k, v, None)
+    for k, (_, v, level) in enumerate(blocks):
+        coarse_forward(NETS + k, v, level, False)
     sums = [csums[k] + part for k, part in enumerate(coarse_sums(blocks, NETS))]
-    s_one, s_curve = sums[2][0:1], sums[0][12:13]
-    moments = co * (2.0 * squares * sums[1][8:13] - 4.0 * ci[3:4] * sums[0][0:5])
+    moments, s_one, s_curve = sums[0][0:5], sums[1][0:1], sums[2][0:1]
     extra = jnp.concatenate(
         [
             (4.0 * scales[0] * scales[0]) * ci[0:1] * co * s_curve,
@@ -695,7 +695,7 @@
         backward(n, (0,), [eown[n, 0:1, :]], False)
         return carry
 
-    lax.fori_loop(0, NETS, own_backward, 0)
+    lax.fori_loop(0, NETS, own_backward, 0, unroll=4)
     hear(2, (0,))
     ar_start(1, ar_finish(0))
 
@@ -752,7 +752,7 @@
         flat_out[n, 67:68, 64:128] = last
         return carry
 
-    lax.fori_loop(0, NETS, face_backward, 0)
+    lax.fori_loop(0, NETS, face_backward, 0, unroll=2)
     count = NETS * sizes[0] * sizes[1] * sizes[2]
     for n in range(NETS):
         grad_out[n // 2, :, n % 2, :] = flat_out[n]
@@ -842,10 +842,11 @@
             pltpu.VMEM((NETS, 16, PTS), F32),
             pltpu.VMEM((HID, PTS), F32),
             pltpu.VMEM((NETS, 8, PTS), F32),
-            pltpu.VMEM((2, COARSE, PTS), F32),
-            pltpu.VMEM((4, COARSE, 10 * PTS), BF),
+            pltpu.VMEM((3, COARSE, PTS), F32),
+            pltpu.VMEM((2, COARSE, 10 * PTS), BF),
             pltpu.VMEM((COARSE, 10 * PTS), F32),
-            pltpu.VMEM((3, 16, COARSE), F32),
+            pltpu.VMEM((COARSE, 10 * PTS), F32),
+            pltpu.VMEM((3, 8, COARSE), F32),
             pltpu.VMEM((2, 16, 24, PTS), F32),
             pltpu.SemaphoreType.DMA((6,)),
             pltpu.SemaphoreType.DMA((6,)),

time: 35.6 us -> 33.2 us (0.933)
  Pallas kernels: 34.8 us -> 32.4 us
    pallas_call x1, Pallas kernels: 33.2 us -> 30.8 us  [on_device(): pl.pallas_call(partial(kernel, sizes), out_shape=(jax.ShapeDtypeStruct((N...]
where the time goes in v2:
time: 33.2 us; the launch traced here: 33 us
  Pallas kernels  32.4 us (98%)
  between operations  0.64 us (2%)
    pallas_call x1, Pallas kernels, on_device(): pl.pallas_call(partial(kernel, sizes), out_shape=(jax.ShapeDtypeStruct((N...  30.8 us
    pallas_call x1, Pallas kernels, on_device(): pl.pallas_call(writer, out_shape=tuple((jax.ShapeDtypeStruct(value.shape,...  1.58 us

profile of v2, /device:TPU:1, one launch (start us, length us, event | category | flops | bytes accessed | tf_op | source)
XLA Modules:
  0.0 33.0 jit_solution(9145586937042692590)
XLA Ops:
  0.6 30.8 %shard_map.102 = (f32[4,128]{1,0:T(4,128)}, f32[2,68,2,128]{3,2,1,0:T(2,128)}, f32[5,512]{1,0:T(8,128)}, f32[1,512]{1,0:T(1,128)}) custom-call(f32[2,68,2,128]{3,2,1,0:T(2,128)} %bitcast.15, f32[5,512]{1,0:T(8,128)} %inner_hbm.1, f32[1,512]{1,0:T(1,128)} %bitcast.18, f32[4,4,128]{2,1,0:T(4,128)} %bitcast.17, f32[4,128]{1,0:T(4,128)} %bitcast.19, ...), custom_call_target="tpu_custom_call" | custom-call | tf_op jit(solution)/shard_map/pallas_call | solution.py:795
  31.4 1.6 %shard_map.103 = (f32[4,128]{1,0:T(4,128)}, f32[2,68,2,128]{3,2,1,0:T(2,128)}, f32[5,512]{1,0:T(8,128)}, f32[1,512]{1,0:T(1,128)}) custom-call(f32[4,128]{1,0:T(4,128)} %get-tuple-element.12.refs_0_, f32[2,68,2,128]{3,2,1,0:T(2,128)} %get-tuple-element.13.refs_1_, f32[5,512]{1,0:T(8,128)} %get-tuple-element.14.refs_2_, f32[1,512]{1,0:T(1,128)} %get-tuple-element.15.refs_3_), custom_call_target="tpu_custom_call" | custom-call | tf_op jit(solution)/shard_map/pallas_call | solution.py:874

commit v3 on v2

--- a/solution.py
+++ b/solution.py
@@ -154,24 +154,44 @@
         (place[0], sizes[0], lambda p: {"gx": p}),
     ]
 
+    def partners(stage):
+        pos, size, _ = groups[stage]
+        if sizes != (16, 4, 4):
+            return [lax.rem(pos + k, size) for k in range(1, size)]
+        if stage == 1:
+            steps = [(2 * a + min(z, 8 - z), a, z) for a in range(2) for z in range(8)]
+            return [
+                lax.rem(pos // 8 + a, 2) * 8 + lax.rem(pos + z, 8)
+                for hops, a, z in sorted(steps, reverse=True)
+                if hops
+            ]
+        steps = [
+            (4 * a + 4 * min(y, 4 - y) + b, a, b, y)
+            for a in range(2)
+            for b in range(2)
+            for y in range(4)
+        ]
+        return [
+            lax.rem(place[1] // 2 + a, 2) * 8 + lax.rem(place[1] + b, 2) * 4 + lax.rem(place[2] + y, 4)
+            for hops, a, b, y in sorted(steps, reverse=True)
+            if hops
+        ]
+
     def ring(axis, step):
         return {AXES[axis]: lax.rem(place[axis] + step + sizes[axis], sizes[axis])}
 
-    def pass_on(level, axes):
-        for axis in axes:
-            reach = (1 << level) if axis == 0 else 1
-            for side in range(2):
-                pl.semaphore_signal(
-                    tokens.at[level, 2 * axis + side],
-                    inc=1,
-                    device_id=ring(axis, reach if side else -reach),
-                    device_id_type=MESH,
-                )
-
-    def hear(level, axes):
-        for axis in axes:
-            for side in range(2):
-                pl.semaphore_wait(tokens.at[level, 2 * axis + side], 1)
+    def pass_on(level):
+        for side in range(2):
+            pl.semaphore_signal(
+                tokens.at[level, side],
+                inc=1,
+                device_id=ring(0, (1 << level) if side else -(1 << level)),
+                device_id_type=MESH,
+            )
+
+    def hear(level):
+        for side in range(2):
+            pl.semaphore_wait(tokens.at[level, side], 1)
 
     def exchange(source_of, landing, send_sem, recv_sem, flip):
         for slot in range(6):
@@ -207,9 +227,8 @@
                 ).wait_send()
 
     def ar_copies(stage, arriving):
-        pos, size, member = groups[stage]
-        for k in range(1, size):
-            partner = lax.rem(pos + k, size)
+        pos, _, member = groups[stage]
+        for partner in partners(stage):
             slot = partner if arriving else pos
             yield pltpu.make_async_remote_copy(
                 ar.at[stage, pos], ar.at[stage, slot],
@@ -235,9 +254,13 @@
     rin[...] = jnp.zeros_like(rin)
 
     barrier = pltpu.get_barrier_semaphore()
-    for axis in range(3):
-        for step in (-1, 1):
-            pl.semaphore_signal(barrier, inc=1, device_id=ring(axis, step), device_id_type=MESH)
+    for step in (-1, 1):
+        pl.semaphore_signal(barrier, inc=1, device_id=ring(0, step), device_id_type=MESH)
+    pos, size, member = groups[0]
+    for k in range(1, size):
+        pl.semaphore_signal(
+            barrier, inc=1, device_id=member(lax.rem(pos + k, size)), device_id_type=MESH
+        )
 
     fetches = [
         pltpu.make_async_copy(far, near, in_sem.at[k])
@@ -282,10 +305,10 @@
         gbuf[0, j] = moved[:, 0:PTS] - shift_a
         gbuf[1, j] = moved[:, PTS : 2 * PTS] - shift_b
 
-    pl.semaphore_wait(barrier, 6)
+    pl.semaphore_wait(barrier, 2 + groups[0][1] - 1)
     g_args = (lambda slot: gbuf.at[slot // 4], gin, g_send, g_recv, False)
     exchange(*g_args)
-    pass_on(0, (0, 1, 2))
+    pass_on(0)
 
     for fetch in fetches[3:]:
         fetch.wait()
@@ -294,9 +317,9 @@
         flat = params[n // 2, :, n % 2, :]
         even = pltpu.roll(jnp.where(half, flat[35:67], flat[2:34]), HID, 1)
         odd = jnp.where(half, flat[3:35], flat[35:67])
-        work[pl.ds(0, 32, stride=2), :] = even
-        work[pl.ds(1, 32, stride=2), :] = odd
-        both = work[...]
+        work[n, pl.ds(0, 32, stride=2), :] = even
+        work[n, pl.ds(1, 32, stride=2), :] = odd
+        both = work[n]
         hi, lo = split2(both)
         lb[n, 0, :, 0:64] = hi[:, 0:64]
         lb[n, 0, :, 64:128] = hi[:, 0:64]
@@ -420,14 +443,14 @@
             one = out * one
             two = -2.0 * hidden * one
             curved = coef[5] * (z1 * z1 + z2 * z2 + z3 * z3)
-            put(dz, 0, at, coef[0] * one + two * (mixed * row) + (out * three) * curved)
+            put(dz, 3 * n + 0, at, coef[0] * one + two * (mixed * row) + (out * three) * curved)
             twice = 2.0 * coef[5] * two
             for k, z in ((1, z1), (2, z2), (3, z3)):
-                put(dz, 0, at + k * PTS, coef[k] * one + twice * z)
-            put(dz, 0, at + 4 * PTS, coef[4] * one)
-            put(dz, 0, at + 5 * PTS, coef[5] * one)
-        product = dot(lb[n, 1], dz[0, 0:192, begin:end])
-        collect(acc3, dot_nt(act2[n, 64:208, begin:end], dz[0, 0:128, begin:end]))
+                put(dz, 3 * n + 0, at + k * PTS, coef[k] * one + twice * z)
+            put(dz, 3 * n + 0, at + 4 * PTS, coef[4] * one)
+            put(dz, 3 * n + 0, at + 5 * PTS, coef[5] * one)
+        product = dot(lb[n, 1], dz[3 * n + 0, 0:192, begin:end])
+        collect(acc3, dot_nt(act2[n, 64:208, begin:end], dz[3 * n + 0, 0:128, begin:end]))
         row = jnp.concatenate(rows, axis=1)
         span = slice(tiles[0] * PTS, (tiles[-1] + 1) * PTS)
         collect(acco, dot_nt(stacked3(row), qs[n, :, span]))
@@ -443,14 +466,14 @@
             for k in range(1, 5):
                 mixed = mixed + z[k] * a[k]
             curved = (z[1] * z[1] + z[2] * z[2] + z[3] * z[3]) * a[5]
-            put(dz, 1, at, one * a[0] + two * mixed + three * curved)
+            put(dz, 3 * n + 1, at, one * a[0] + two * mixed + three * curved)
             twice = 2.0 * two * a[5]
             for k in range(1, 4):
-                put(dz, 1, at + k * PTS, one * a[k] + twice * z[k])
-            put(dz, 1, at + 4 * PTS, one * a[4])
-            put(dz, 1, at + 5 * PTS, one * a[5])
-        product = dot(lb[n, 0], dz[1, 0:192, begin:end])
-        collect(acc2, dot_nt(act1[n, 64:208, begin:end], dz[1, 0:128, begin:end]))
+                put(dz, 3 * n + 1, at + k * PTS, one * a[k] + twice * z[k])
+            put(dz, 3 * n + 1, at + 4 * PTS, one * a[4])
+            put(dz, 3 * n + 1, at + 5 * PTS, one * a[5])
+        product = dot(lb[n, 0], dz[3 * n + 1, 0:192, begin:end])
+        collect(acc2, dot_nt(act1[n, 64:208, begin:end], dz[3 * n + 1, 0:128, begin:end]))
         total = None
         for tile in tiles:
             at = tile * WIDTH
@@ -465,10 +488,10 @@
                 mixed = mixed + wide[n, k] * a[k + 1]
             twice = 2.0 * two * a[5]
             base = tile * WIDTH
-            put(dz, 2, base, one * a[0] + two * mixed + three * (wsq[n] * a[5]))
+            put(dz, 3 * n + 2, base, one * a[0] + two * mixed + three * (wsq[n] * a[5]))
             for k in range(3):
-                put(dz, 2, base + (k + 1) * PTS, one * a[k + 1] + twice * wide[n, k])
-            put(dz, 2, base + 4 * PTS, one * a[4])
+                put(dz, 3 * n + 2, base + (k + 1) * PTS, one * a[k + 1] + twice * wide[n, k])
+            put(dz, 3 * n + 2, base + 4 * PTS, one * a[4])
             x = xs[n, tile]
             hi = x.astype(BF).astype(F32)
             top = jnp.where(row8 < 4, hi, jnp.where(row8 == 4, 1.0, 0.0))
@@ -477,7 +500,7 @@
             for k in range(4):
                 pieces.append(jnp.where(iota((16, PTS), 0) == k, 1.0, 0.0))
             left = jnp.concatenate(pieces, axis=1).astype(BF)
-            part = dot_nt(left, dz[2, 0:128, base : base + 5 * PTS])
+            part = dot_nt(left, dz[3 * n + 2, 0:128, base : base + 5 * PTS])
             total = part if total is None else total + part
         collect(acc1, total)
 
@@ -573,10 +596,10 @@
     for k in range(3):
         csums[k] = own_sums[k]
 
-    hear(0, (0, 1, 2))
-    pass_on(1, (0, 1, 2))
 
     arrive(*g_args)
+    hear(0)
+    pass_on(1)
     def choose(parts):
         picked = parts[-1]
         for k in range(len(parts) - 2, -1, -1):
@@ -600,6 +623,21 @@
         ]
         xs[n, 2] = choose(slots)
 
+    def joined_halves(first, second):
+        return jnp.where(lane < HID, first, pltpu.roll(second, HID, 1))
+
+    def face_block(n, tile):
+        x = xs[n, tile]
+        return coarse_inputs(n, x), x[4:5]
+
+    face_blocks = [face_block(n, 1) for n in range(NETS)]
+    for n in range(0, NETS, 2):
+        face_blocks.append(
+            tuple(map(joined_halves, face_block(n, 2), face_block(n + 1, 2)))
+        )
+    for k, (v, level) in enumerate(face_blocks):
+        coarse_forward(NETS + k, v, level, False)
+
     def face_forward(n, carry):
         first, second = forward(n, (1, 2))
         ebuf[0, pl.ds(n, 1), :] = first
@@ -607,35 +645,21 @@
         return carry
 
     ebuf[...] = jnp.zeros_like(ebuf)
-    lax.fori_loop(0, 2, face_forward, 0, unroll=2)
-    hear(1, (1, 2))
-    pass_on(2, (1, 2))
-    lax.fori_loop(2, NETS, face_forward, 0, unroll=2)
+    lax.fori_loop(0, NETS, face_forward, 0, unroll=4)
     e_args = (lambda slot: ebuf.at[slot // 4], ein, e_send, e_recv, True)
     exchange(*e_args)
 
-    hear(1, (0,))
-    pass_on(2, (0,))
-    def joined_halves(first, second):
-        return jnp.where(lane < HID, first, pltpu.roll(second, HID, 1))
-
-    weights, inputs, levels = [], [], []
-    for n in range(NETS):
-        for tile in range(2):
-            x = xs[n, tile + 1]
-            weights.append(ebuf[tile, n : n + 1, :] * x[5:6] * (1.0 / PTS))
-            inputs.append(coarse_inputs(n, x))
-            levels.append(x[4:5])
-    blocks = [(weights[2 * n], inputs[2 * n], levels[2 * n]) for n in range(NETS)]
-    for n in range(0, NETS, 2):
-        blocks.append(
-            tuple(
-                joined_halves(values[2 * n + 1], values[2 * n + 3])
-                for values in (weights, inputs, levels)
-            )
-        )
-    for k, (_, v, level) in enumerate(blocks):
-        coarse_forward(NETS + k, v, level, False)
+    weights = [
+        [
+            ebuf[tile, n : n + 1, :] * xs[n, tile + 1, 5:6, :] * (1.0 / PTS)
+            for tile in range(2)
+        ]
+        for n in range(NETS)
+    ]
+    weights = [pair[0] for pair in weights] + [
+        joined_halves(weights[n][1], weights[n + 1][1]) for n in range(0, NETS, 2)
+    ]
+    blocks = [(weight, v, level) for weight, (v, level) in zip(weights, face_blocks)]
     sums = [csums[k] + part for k, part in enumerate(coarse_sums(blocks, NETS))]
     moments, s_one, s_curve = sums[0][0:5], sums[1][0:1], sums[2][0:1]
     extra = jnp.concatenate(
@@ -650,11 +674,13 @@
     )
     outer_grad = 2.0 * ci[3:4] * s_one + 2.0 * squares * s_curve
     partial_sums = jnp.concatenate([moments + extra, outer_grad], axis=0)
-    hear(2, (1, 2))
     ar_start(
         0,
         jnp.concatenate([partial_sums[:, k * PTS : (k + 1) * PTS] for k in range(4)], axis=0),
     )
+
+    hear(1)
+    pass_on(2)
 
     arrive(*e_args)
     for j in range(NETS):
@@ -691,17 +717,27 @@
     r_args = (lambda slot: rbuf.at[slot // 4], rin, r_send, r_recv, False)
     exchange(*r_args)
 
+    hear(2)
+    ar_start(1, ar_finish(0))
+
     def own_backward(n, carry):
         backward(n, (0,), [eown[n, 0:1, :]], False)
         return carry
 
     lax.fori_loop(0, NETS, own_backward, 0, unroll=4)
-    hear(2, (0,))
-    ar_start(1, ar_finish(0))
 
     arrive(*r_args)
     for n in range(NETS):
         b, c = n // 2, n % 2
+        second = choose(
+            [
+                rbuf[1, n + 1 : n + 2, :] if c == 0 else rin[4, n - 1 : n, :],
+                rbuf[1, n - 1 : n, :] if c == 1 else rin[5, n + 1 : n + 2, :],
+                jnp.zeros((1, PTS), F32),
+            ]
+        )
+        cols[n, 1] = jnp.broadcast_to(second, (8, PTS))
+
         first = choose(
             [
                 rin[0, n : n + 1, :],
@@ -710,15 +746,7 @@
                 rbuf[0, n - 2 : n - 1, :] if b == 1 else rin[3, n + 2 : n + 3, :],
             ]
         )
-        second = choose(
-            [
-                rbuf[1, n + 1 : n + 2, :] if c == 0 else rin[4, n - 1 : n, :],
-                rbuf[1, n - 1 : n, :] if c == 1 else rin[5, n + 1 : n + 2, :],
-                jnp.zeros((1, PTS), F32),
-            ]
-        )
         cols[n, 0] = jnp.broadcast_to(first, (8, PTS))
-        cols[n, 1] = jnp.broadcast_to(second, (8, PTS))
 
     def face_backward(n, carry):
         backward(n, (1, 2), [cols[n, 0, 0:1, :], cols[n, 1, 0:1, :]], True)
@@ -727,9 +755,9 @@
             low_rows = ref[n, 0:64, :]
             high_rows = ref[n, 64:128, :]
             joined.append(low_rows[:, 0:64] + high_rows[:, 0:64] + high_rows[:, 64:128])
-        work[...] = jnp.concatenate(joined, axis=1)
-        even = work[pl.ds(0, 32, stride=2), :]
-        odd = work[pl.ds(1, 32, stride=2), :]
+        work[n] = jnp.concatenate(joined, axis=1)
+        even = work[n, pl.ds(0, 32, stride=2), :]
+        odd = work[n, pl.ds(1, 32, stride=2), :]
         bias2 = acc2[n, 128:129, :]
         bias3 = acc3[n, 128:129, :]
         bias2 = bias2[:, 0:64] + bias2[:, 64:128]
@@ -752,7 +780,7 @@
         flat_out[n, 67:68, 64:128] = last
         return carry
 
-    lax.fori_loop(0, NETS, face_backward, 0, unroll=2)
+    lax.fori_loop(0, NETS, face_backward, 0, unroll=4)
     count = NETS * sizes[0] * sizes[1] * sizes[2]
     for n in range(NETS):
         grad_out[n // 2, :, n % 2, :] = flat_out[n]
@@ -835,12 +863,12 @@
             pltpu.VMEM((NETS, HID, 3 * WIDTH), F32),
             pltpu.VMEM((NETS, HID, 3 * WIDTH), F32),
             pltpu.VMEM((NETS, PTS, 3 * PTS), BF),
-            pltpu.VMEM((3, 192, 3 * WIDTH), BF),
+            pltpu.VMEM((3 * NETS, 192, 3 * WIDTH), BF),
             pltpu.VMEM((NETS, 144, PTS), F32),
             pltpu.VMEM((NETS, 144, PTS), F32),
             pltpu.VMEM((NETS, 16, PTS), F32),
             pltpu.VMEM((NETS, 16, PTS), F32),
-            pltpu.VMEM((HID, PTS), F32),
+            pltpu.VMEM((NETS, HID, PTS), F32),
             pltpu.VMEM((NETS, 8, PTS), F32),
             pltpu.VMEM((3, COARSE, PTS), F32),
             pltpu.VMEM((2, COARSE, 10 * PTS), BF),
@@ -856,7 +884,7 @@
             pltpu.SemaphoreType.DMA((6,)),
             pltpu.SemaphoreType.DMA((2, 16)),
             pltpu.SemaphoreType.DMA((2, 16)),
-            pltpu.SemaphoreType.REGULAR((3, 6)),
+            pltpu.SemaphoreType.REGULAR((3, 2)),
             pltpu.VMEM((NETS, ROWS, PTS), F32),
         ],
         compiler_params=pltpu.CompilerParams(

time: 33.2 us -> 32.2 us (0.970)
  the two profiles are of different devices: /device:TPU:1 before, /device:TPU:6 now
where the time goes in v3:
time: 32.2 us; the launch traced here: 32 us
  Pallas kernels  31.4 us (98%)
  between operations  0.64 us (2%)
    pallas_call x1, Pallas kernels, on_device(): pl.pallas_call(partial(kernel, sizes), out_shape=(jax.ShapeDtypeStruct((N...  29.8 us
    pallas_call x1, Pallas kernels, on_device(): pl.pallas_call(writer, out_shape=tuple((jax.ShapeDtypeStruct(value.shape,...  1.58 us

profile of v3, /device:TPU:6, one launch (start us, length us, event | category | flops | bytes accessed | tf_op | source)
XLA Modules:
  0.0 32.0 jit_solution(18372120766033406748)
XLA Ops:
  0.6 29.8 %shard_map.102 = (f32[4,128]{1,0:T(4,128)}, f32[2,68,2,128]{3,2,1,0:T(2,128)}, f32[5,512]{1,0:T(8,128)}, f32[1,512]{1,0:T(1,128)}) custom-call(f32[2,68,2,128]{3,2,1,0:T(2,128)} %bitcast.15, f32[5,512]{1,0:T(8,128)} %inner_hbm.1, f32[1,512]{1,0:T(1,128)} %bitcast.18, f32[4,4,128]{2,1,0:T(4,128)} %bitcast.17, f32[4,128]{1,0:T(4,128)} %bitcast.19, ...), custom_call_target="tpu_custom_call" | custom-call | tf_op jit(solution)/shard_map/pallas_call | solution.py:823
  30.4 1.6 %shard_map.103 = (f32[4,128]{1,0:T(4,128)}, f32[2,68,2,128]{3,2,1,0:T(2,128)}, f32[5,512]{1,0:T(8,128)}, f32[1,512]{1,0:T(1,128)}) custom-call(f32[4,128]{1,0:T(4,128)} %get-tuple-element.12.refs_0_, f32[2,68,2,128]{3,2,1,0:T(2,128)} %get-tuple-element.13.refs_1_, f32[5,512]{1,0:T(8,128)} %get-tuple-element.14.refs_2_, f32[1,512]{1,0:T(1,128)} %get-tuple-element.15.refs_3_), custom_call_target="tpu_custom_call" | custom-call | tf_op jit(solution)/shard_map/pallas_call | solution.py:902

commit v4 on v3

--- a/solution.py
+++ b/solution.py
@@ -249,19 +249,6 @@
             total = total + ar[stage, p]
         return total
 
-    gin[...] = jnp.zeros_like(gin)
-    ein[...] = jnp.zeros_like(ein)
-    rin[...] = jnp.zeros_like(rin)
-
-    barrier = pltpu.get_barrier_semaphore()
-    for step in (-1, 1):
-        pl.semaphore_signal(barrier, inc=1, device_id=ring(0, step), device_id_type=MESH)
-    pos, size, member = groups[0]
-    for k in range(1, size):
-        pl.semaphore_signal(
-            barrier, inc=1, device_id=member(lax.rem(pos + k, size)), device_id_type=MESH
-        )
-
     fetches = [
         pltpu.make_async_copy(far, near, in_sem.at[k])
         for k, (far, near) in enumerate(
@@ -278,6 +265,19 @@
     ]
     for fetch in fetches:
         fetch.start()
+
+    gin[...] = jnp.zeros_like(gin)
+    ein[...] = jnp.zeros_like(ein)
+    rin[...] = jnp.zeros_like(rin)
+
+    barrier = pltpu.get_barrier_semaphore()
+    for step in (-1, 1):
+        pl.semaphore_signal(barrier, inc=1, device_id=ring(0, step), device_id_type=MESH)
+    pos, size, member = groups[0]
+    for k in range(1, size):
+        pl.semaphore_signal(
+            barrier, inc=1, device_id=member(lax.rem(pos + k, size)), device_id_type=MESH
+        )
 
     lane = iota((1, PTS), 1)
     row8 = iota((8, PTS), 0)
@@ -782,29 +782,31 @@
 
     lax.fori_loop(0, NETS, face_backward, 0, unroll=4)
     count = NETS * sizes[0] * sizes[1] * sizes[2]
-    for n in range(NETS):
-        grad_out[n // 2, :, n % 2, :] = flat_out[n]
     stores = [
         pltpu.make_async_copy(near, away, out_sem.at[k])
         for k, (near, away) in enumerate(
             (
                 (res_out, res_far),
-                (grad_out, grad_far),
+                (grad_out.at[0], grad_far.at[0]),
+                (grad_out.at[1], grad_far.at[1]),
                 (inner_out, inner_far),
                 (outer_out, outer_far),
             )
         )
     ]
     stores[0].start()
-    stores[1].start()
+    for b in range(2):
+        for c in range(2):
+            grad_out[b, :, c, :] = flat_out[2 * b + c]
+        stores[1 + b].start()
     for args in (g_args, e_args, r_args):
         sent(*args)
     total = ar_finish(1) * (count ** (-0.5))
     for k in range(4):
         inner_out[:, k * PTS : (k + 1) * PTS] = total[6 * k : 6 * k + 5]
         outer_out[:, k * PTS : (k + 1) * PTS] = total[6 * k + 5 : 6 * k + 6]
-    stores[2].start()
     stores[3].start()
+    stores[4].start()
     for store in stores:
         store.wait()
     for stage in range(2):
@@ -835,7 +837,7 @@
             pltpu.VMEM((2, ROWS, 2, PTS), F32),
             pltpu.VMEM((5, COARSE), F32),
             pltpu.VMEM((1, COARSE), F32),
-            pltpu.SemaphoreType.DMA((4,)),
+            pltpu.SemaphoreType.DMA((5,)),
             pltpu.VMEM((2, ROWS, 2, PTS), F32),
             pltpu.VMEM((5, COARSE), F32),
             pltpu.VMEM((1, COARSE), F32),

time: 32.2 us -> 32.2 us (level)
  no operation moved by 1% of the time
where the time goes in v4:
time: 32.2 us; the launch traced here: 32.1 us
  Pallas kernels  31.4 us (98%)
  between operations  0.64 us (2%)
    pallas_call x1, Pallas kernels, on_device(): pl.pallas_call(partial(kernel, sizes), out_shape=(jax.ShapeDtypeStruct((N...  29.8 us
    pallas_call x1, Pallas kernels, on_device(): pl.pallas_call(writer, out_shape=tuple((jax.ShapeDtypeStruct(value.shape,...  1.58 us

profile of v4, /device:TPU:6, one launch (start us, length us, event | category | flops | bytes accessed | tf_op | source)
XLA Modules:
  0.0 32.1 jit_solution(16618323998896750807)
XLA Ops:
  0.6 29.8 %shard_map.102 = (f32[4,128]{1,0:T(4,128)}, f32[2,68,2,128]{3,2,1,0:T(2,128)}, f32[5,512]{1,0:T(8,128)}, f32[1,512]{1,0:T(1,128)}) custom-call(f32[2,68,2,128]{3,2,1,0:T(2,128)} %bitcast.15, f32[5,512]{1,0:T(8,128)} %inner_hbm.1, f32[1,512]{1,0:T(1,128)} %bitcast.18, f32[4,4,128]{2,1,0:T(4,128)} %bitcast.17, f32[4,128]{1,0:T(4,128)} %bitcast.19, ...), custom_call_target="tpu_custom_call" | custom-call | tf_op jit(solution)/shard_map/pallas_call | solution.py:825
  30.5 1.6 %shard_map.103 = (f32[4,128]{1,0:T(4,128)}, f32[2,68,2,128]{3,2,1,0:T(2,128)}, f32[5,512]{1,0:T(8,128)}, f32[1,512]{1,0:T(1,128)}) custom-call(f32[4,128]{1,0:T(4,128)} %get-tuple-element.12.refs_0_, f32[2,68,2,128]{3,2,1,0:T(2,128)} %get-tuple-element.13.refs_1_, f32[5,512]{1,0:T(8,128)} %get-tuple-element.14.refs_2_, f32[1,512]{1,0:T(1,128)} %get-tuple-element.15.refs_3_), custom_call_target="tpu_custom_call" | custom-call | tf_op jit(solution)/shard_map/pallas_call | solution.py:904
